TPU v7x, 512 devices: a whole 4x4x16 slice. The times are simulated.
512 devices in a mesh: sim: 32 (over z_lo, y, core), grp: 4 (over z_hi), gz: 4 (over x).
Axes of the slice: x: 4, y: 4, z: 16 (z_hi: 4, z_lo: 4; z = z_hi * 4 + z_lo), core: 2. Of those that a mesh axis runs over, the one named last changes fastest.
Arguments:
- fields: float32 [8, 2, 1024, 1024], P(None, None, 'sim', ('grp', 'gz')), may hold values from -6 to 6
- diffusivity: float32 [8], replicated, may hold values from 0.03 to 0.12
- velocity: float32 [2, 8], replicated, may hold values from -0.4 to 0.4
- coupling: float32 [8, 8], replicated, may hold values from -0.6 to 0.6
- basis_x: bfloat16 [1024, 128], replicated, may hold values from -0.1875 to 0.1875
- basis_y: bfloat16 [1024, 128], replicated, may hold values from -0.1875 to 0.1875
Outputs:
- fields_out: float32 [8, 2, 1024, 1024], P(None, None, 'sim', ('grp', 'gz'))
- gram_x: float32 [1024, 1024], P('sim', ('grp', 'gz'))
- gram_y: float32 [1024, 1024], P(('grp', 'gz'), 'sim')
- core: float32 [8, 2, 128, 128], P(None, None, 'sim', ('grp', 'gz'))
All inputs are finite; a program needn't handle non-finite values.
Results may differ from a plain program's by a relative error of at most 0.0003.
Values sent between devices are 32-bit elements; how exact they have to be, the bound alone decides.
A program may use at most 64 MiB of HBM per device.

v0:
```python
import jax
import jax.numpy as jnp
from jax import lax
from jax.sharding import PartitionSpec as P

NY = 1024
RANK = 128
STEPS = 2


time_step = 1.0
highest = lax.Precision.HIGHEST


def with_halo(cells, sides, width):
    for axis, dim in sides:
        count = lax.axis_size(axis)
        head = lax.slice_in_dim(cells, 0, width, axis=dim)
        tail = lax.slice_in_dim(cells, cells.shape[dim] - width, cells.shape[dim], axis=dim)
        cells = jnp.concatenate(
            [
                lax.ppermute(tail, axis, [(i, (i + 1) % count) for i in range(count)]),
                cells,
                lax.ppermute(head, axis, [((i + 1) % count, i) for i in range(count)]),
            ],
            axis=dim,
        )
    return cells


def rates(state, diffusivity, velocity, coupling):
    padded = with_halo(state, (("sim", 2), (("grp", "gz"), 3)), 1)
    center = padded[:, :, 1:-1, 1:-1]
    x_plus = padded[:, :, 2:, 1:-1]
    x_minus = padded[:, :, :-2, 1:-1]
    y_plus = padded[:, :, 1:-1, 2:]
    y_minus = padded[:, :, 1:-1, :-2]
    z_plus = jnp.roll(center, -1, 1)
    z_minus = jnp.roll(center, 1, 1)
    lapl = -6.0 * center + z_plus + z_minus + x_plus + x_minus + y_plus + y_minus
    grad_x = (x_plus - x_minus) * 0.5
    grad_y = (y_plus - y_minus) * 0.5
    react = jnp.einsum("fg,gzxy->fzxy", coupling, jnp.tanh(center), precision=highest)
    return (
        diffusivity[:, None, None, None] * lapl
        - velocity[0][:, None, None, None] * grad_x
        - velocity[1][:, None, None, None] * grad_y
        + react
    )


def shards(fields, diffusivity, velocity, coupling, basis_x, basis_y):
    state = fields
    for repeat in range(STEPS):
        first = rates(state, diffusivity, velocity, coupling)
        second = rates(state + 0.5 * time_step * first, diffusivity, velocity, coupling)
        third = rates(state + 0.5 * time_step * second, diffusivity, velocity, coupling)
        fourth = rates(state + time_step * third, diffusivity, velocity, coupling)
        state = state + time_step / 6.0 * (first + 2.0 * second + 2.0 * third + fourth)
    nfield = state.shape[0]
    depth = state.shape[1]
    x_rows = state.shape[2]
    y_cols = state.shape[3]
    basis_xf = basis_x.astype(jnp.float32)
    basis_yf = basis_y.astype(jnp.float32)
    block = jnp.einsum(
        "fzxy,fzwy->xw", state, lax.all_gather(state, "sim", axis=2, tiled=True), precision=highest
    )
    gram_rows = block
    own_basis = lax.dynamic_slice_in_dim(basis_xf, lax.axis_index("sim") * x_rows, x_rows, 0)
    partial_proj = jnp.einsum("xr,fzxy->fzry", own_basis, state, precision=highest)
    projected = lax.psum_scatter(partial_proj, "sim", scatter_dimension=2, tiled=True)
    gram_x = lax.psum_scatter(gram_rows, ("grp", "gz"), scatter_dimension=1, tiled=True) / (
        nfield * depth * NY
    )
    block = jnp.einsum(
        "fzry,fzrv->yv",
        projected,
        lax.all_gather(projected, ("grp", "gz"), axis=3, tiled=True),
        precision=highest,
    )
    own_basis_y = lax.dynamic_slice_in_dim(
        basis_yf, lax.axis_index(("grp", "gz")) * y_cols, y_cols, 0
    )
    partial_core = jnp.einsum("ys,fzry->fzrs", own_basis_y, projected, precision=highest)
    core = lax.psum_scatter(partial_core, ("grp", "gz"), scatter_dimension=3, tiled=True)
    gram_y = lax.psum_scatter(block, "sim", scatter_dimension=1, tiled=True) / (
        nfield * depth * RANK
    )
    return (state, gram_x, gram_y, core)


def solution(mesh):
    in_specs = (P(None, None, "sim", ("grp", "gz")), P(), P(), P(), P(), P())
    out_specs = (
        P(None, None, "sim", ("grp", "gz")),
        P("sim", ("grp", "gz")),
        P(("grp", "gz"), "sim"),
        P(None, None, "sim", ("grp", "gz")),
    )
    return jax.shard_map(shards, mesh=mesh, in_specs=in_specs, out_specs=out_specs, check_vma=False)
```

profile of v0, /device:TPU:1, one launch (start us, length us, event | category | flops | bytes accessed | tf_op | source)
XLA Modules:
  0.0 979.0 jit_solution(15464868327093606342)
XLA Ops:
  8.5 4.6 collective-permute-start.1
  13.1 6.1 collective-permute-start
  22.4 12.6 %collective-permute-start.2 = (f32[8,2,34,1]{3,0,2,1:T(8,128)S(1)}, f32[8,2,34,1]{3,0,2,1:T(8,128)S(1)}, u32[]{:S(2)}, u32[]{:S(2)}) collective-permute-start(f32[8,2,34,1]{3,0,2,1:T(8,128)S(1)} %get-tuple-element.31), channel_id=1, source_target_pairs={{1,0},{2,1},{3,2},{4,3},{5,4},{6,5},{7,6},{8,7},{9,8},{10,9},{11,1... | collective-permute-start | bytes 6536 | tf_op jit(solution)/shard_map/ppermute | solution.py:24
  37.3 20.5 %collective-permute-done.2 = f32[8,2,34,1]{3,0,2,1:T(8,128)S(1)} collective-permute-done((f32[8,2,34,1]{3,0,2,1:T(8,128)S(1)}, f32[8,2,34,1]{3,0,2,1:T(8,128)S(1)}, u32[]{:S(2)}, u32[]{:S(2)}) %collective-permute-start.2) | collective-permute-done | bytes 2208 | tf_op jit(solution)/shard_map/ppermute | solution.py:24
  69.9 9.8 %collective-permute-start.6 = (f32[8,2,34,1]{3,0,2,1:T(8,128)S(1)}, f32[8,2,34,1]{3,0,2,1:T(8,128)S(1)}, u32[]{:S(2)}, u32[]{:S(2)}) collective-permute-start(f32[8,2,34,1]{3,0,2,1:T(8,128)S(1)} %get-tuple-element.29), channel_id=1, source_target_pairs={{1,0},{2,1},{3,2},{4,3},{5,4},{6,5},{7,6},{8,7},{9,8},{10,9},{11,1... | collective-permute-start | bytes 6536 | tf_op jit(solution)/shard_map/ppermute | solution.py:24
  79.8 4.6 collective-permute-done.7
  84.4 18.9 %collective-permute-done.6 = f32[8,2,34,1]{3,0,2,1:T(8,128)S(1)} collective-permute-done((f32[8,2,34,1]{3,0,2,1:T(8,128)S(1)}, f32[8,2,34,1]{3,0,2,1:T(8,128)S(1)}, u32[]{:S(2)}, u32[]{:S(2)}) %collective-permute-start.6) | collective-permute-done | bytes 2208 | tf_op jit(solution)/shard_map/ppermute | solution.py:24
  114.3 9.4 collective-permute-start.10
  123.7 14.6 %collective-permute-done.11 = f32[8,2,34,1]{3,0,2,1:T(8,128)S(1)} collective-permute-done((f32[8,2,34,1]{3,0,2,1:T(8,128)S(1)}, f32[8,2,34,1]{3,0,2,1:T(8,128)S(1)}, u32[]{:S(2)}, u32[]{:S(2)}) %collective-permute-start.11) | collective-permute-done | bytes 2208 | tf_op jit(solution)/shard_map/ppermute | solution.py:22
  138.9 4.3 collective-permute-start.12
  148.4 9.9 %collective-permute-start.14 = (f32[8,2,34,1]{3,0,2,1:T(8,128)S(1)}, f32[8,2,34,1]{3,0,2,1:T(8,128)S(1)}, u32[]{:S(2)}, u32[]{:S(2)}) collective-permute-start(f32[8,2,34,1]{3,0,2,1:T(8,128)S(1)} %get-tuple-element.25), channel_id=1, source_target_pairs={{1,0},{2,1},{3,2},{4,3},{5,4},{6,5},{7,6},{8,7},{9,8},{10,9},{11,1... | collective-permute-start | bytes 6536 | tf_op jit(solution)/shard_map/ppermute | solution.py:24
  160.2 8.1 collective-permute-done.14
  168.4 16.1 %collective-permute-done.15 = f32[8,2,34,1]{3,0,2,1:T(8,128)S(1)} collective-permute-done((f32[8,2,34,1]{3,0,2,1:T(8,128)S(1)}, f32[8,2,34,1]{3,0,2,1:T(8,128)S(1)}, u32[]{:S(2)}, u32[]{:S(2)}) %collective-permute-start.15) | collective-permute-done | bytes 2208 | tf_op jit(solution)/shard_map/ppermute | solution.py:22
  188.1 5.0 collective-permute-start.17
  195.9 9.4 collective-permute-start.18
  205.3 7.2 collective-permute-done.19
  212.9 5.0 collective-permute-start.20
  224.2 9.4 collective-permute-start.22
  233.6 8.3 collective-permute-done.23
  242.3 4.5 collective-permute-start.24
  252.0 9.9 %collective-permute-start.26 = (f32[8,2,34,1]{3,0,2,1:T(8,128)S(1)}, f32[8,2,34,1]{3,0,2,1:T(8,128)S(1)}, u32[]{:S(2)}, u32[]{:S(2)}) collective-permute-start(f32[8,2,34,1]{3,0,2,1:T(8,128)S(1)} %get-tuple-element.19), channel_id=1, source_target_pairs={{1,0},{2,1},{3,2},{4,3},{5,4},{6,5},{7,6},{8,7},{9,8},{10,9},{11,1... | collective-permute-start | bytes 6536 | tf_op jit(solution)/shard_map/ppermute | solution.py:24
  261.9 11.9 %collective-permute-done.27 = f32[8,2,34,1]{3,0,2,1:T(8,128)S(1)} collective-permute-done((f32[8,2,34,1]{3,0,2,1:T(8,128)S(1)}, f32[8,2,34,1]{3,0,2,1:T(8,128)S(1)}, u32[]{:S(2)}, u32[]{:S(2)}) %collective-permute-start.27) | collective-permute-done | bytes 2208 | tf_op jit(solution)/shard_map/ppermute | solution.py:22
  280.1 12.0 %collective-permute-done.29 = f32[8,2,1,64]{3,0,2,1:T(8,128)S(1)} collective-permute-done((f32[8,2,1,64]{3,0,2,1:T(8,128)S(1)}, f32[8,2,1,64]{3,0,2,1:T(8,128)S(1)}, u32[]{:S(2)}, u32[]{:S(2)}) %collective-permute-start.29) | collective-permute-done | bytes 4128 | tf_op jit(solution)/shard_map/ppermute | solution.py:22
  292.3 10.1 %collective-permute-start.30 = (f32[8,2,34,1]{3,0,2,1:T(8,128)S(1)}, f32[8,2,34,1]{3,0,2,1:T(8,128)S(1)}, u32[]{:S(2)}, u32[]{:S(2)}) collective-permute-start(f32[8,2,34,1]{3,0,2,1:T(8,128)S(1)} %get-tuple-element.17), channel_id=1, source_target_pairs={{1,0},{2,1},{3,2},{4,3},{5,4},{6,5},{7,6},{8,7},{9,8},{10,9},{11,1... | collective-permute-start | bytes 6536 | tf_op jit(solution)/shard_map/ppermute | solution.py:24
  306.1 9.6 collective-permute-done.31
  321.1 173.3 %reduce-scatter.7.cloned.1.call-done = f32[8,2,4,64]{3,0,1,2:T(8,128)} async-done(((f32[8,2,128,64]{3,0,1,2:T(8,128)}), f32[8,2,4,64]{3,0,1,2:T(8,128)}) %reduce-scatter.7.cloned.1.call-update) | async-done | bytes 16400 | tf_op jit(solution)/shard_map/reduce_scatter | solution.py:72
  495.4 211.7 %all_gather.7 = f32[8,2,4,1024]{0,2,1,3:T(4,128)S(1)} all-gather(f32[8,2,4,64]{0,2,1,3:T(4,128)S(1)} %copy.68), channel_id=1, replica_groups=mesh['sim'=32,'grp'=4,'gz'=4] {'grp','gz'}, dimensions={3}, use_global_device_ids=true | all-gather | bytes 278528 | tf_op jit(solution)/shard_map/all_gather | solution.py:79
  707.0 7.6 fusion.4
  715.6 77.3 %all-reduce = f32[8,2,4,128]{3,0,2,1:T(8,128)S(1)} all-reduce(f32[8,2,4,128]{3,0,2,1:T(8,128)S(1)} %fusion.99), channel_id=5, replica_groups=mesh['sim'=32,'grp'=4,'gz'=4] {'grp','gz'}, use_global_device_ids=true, to_apply=%region_3.4.clone | all-reduce | flops 8192 | bytes 65536
  792.8 10.7 %fusion.7 = f32[1024,32]{1,0:T(8,128)} fusion(f32[8,2,32,64]{3,2,1,0:T(8,128)S(1)} %copy.71, f32[8,2,1024,64]{3,0,2,1:T(8,128)} %all-gather.2.cloned.1.call-done), kind=kOutput, calls=%fused_computation.5 | convolution fusion | flops 402653184 | bytes 4456448 | tf_op jit(solution)/shard_map/fzxy,fzwy->xw/dot_general | solution.py:66
  804.3 52.4 %reduce-scatter.9.cloned.1.call-done = f32[64,32]{0,1:T(8,128)} async-done(((f32[64,1024]{0,1:T(8,128)}), f32[64,32]{0,1:T(8,128)}) %reduce-scatter.9.cloned.1.call-update) | async-done | bytes 8208 | tf_op jit(solution)/shard_map/reduce_scatter | solution.py:87
  858.1 112.9 %reduce-scatter.11.cloned.1.call-done = f32[64,32]{1,0:T(8,128)} async-done(((f32[1024,32]{1,0:T(8,128)}), f32[64,32]{1,0:T(8,128)}) %reduce-scatter.11.cloned.1.call-update) | async-done | bytes 8208
  (118 shorter events, 75.9 us)
Async XLA Ops:
  7.2 487.1 %reduce-scatter.7.cloned.1.call-start = ((), (), s32[]{:S(2)}) async-start(), calls=%async_computation.4 | async-start | bytes 1081344 | tf_op jit(solution)/shard_map/reduce_scatter | solution.py:72
  8.5 10.8 %collective-permute-start.1 = (f32[8,2,1,64]{3,0,2,1:T(8,128)S(1)}, f32[8,2,1,64]{3,0,2,1:T(8,128)S(1)}, u32[]{:S(2)}, u32[]{:S(2)}) collective-permute-start(f32[8,2,1,64]{3,0,2,1:T(8,128)S(1)} %get-tuple-element.61), channel_id=1, source_target_pairs={{0,16},{16,32},{32,48},{48,64},{64,80},{80,96},{96,112},{112,128},... | collective-permute-start | bytes 12296 | tf_op jit(solution)/shard_map/ppermute | solution.py:22
  13.1 7.3 collective-permute-start
  20.5 16.8 %collective-permute-start.3 = (f32[8,2,34,1]{3,0,2,1:T(8,128)S(1)}, f32[8,2,34,1]{3,0,2,1:T(8,128)S(1)}, u32[]{:S(2)}, u32[]{:S(2)}) collective-permute-start(f32[8,2,34,1]{3,0,2,1:T(8,128)S(1)} %get-tuple-element.30), channel_id=1, source_target_pairs={{0,1},{1,2},{2,3},{3,4},{4,5},{5,6},{6,7},{7,8},{8,9},{9,10},{10,1... | collective-permute-start | bytes 6536 | tf_op jit(solution)/shard_map/ppermute | solution.py:22
  22.4 35.4 %collective-permute-start.2 = (f32[8,2,34,1]{3,0,2,1:T(8,128)S(1)}, f32[8,2,34,1]{3,0,2,1:T(8,128)S(1)}, u32[]{:S(2)}, u32[]{:S(2)}) collective-permute-start(f32[8,2,34,1]{3,0,2,1:T(8,128)S(1)} %get-tuple-element.31), channel_id=1, source_target_pairs={{1,0},{2,1},{3,2},{4,3},{5,4},{6,5},{7,6},{8,7},{9,8},{10,9},{11,1... | collective-permute-start | bytes 6536 | tf_op jit(solution)/shard_map/ppermute | solution.py:24
  59.4 5.9 collective-permute-start.4
  68.0 16.4 %collective-permute-start.7 = (f32[8,2,34,1]{3,0,2,1:T(8,128)S(1)}, f32[8,2,34,1]{3,0,2,1:T(8,128)S(1)}, u32[]{:S(2)}, u32[]{:S(2)}) collective-permute-start(f32[8,2,34,1]{3,0,2,1:T(8,128)S(1)} %get-tuple-element.28), channel_id=1, source_target_pairs={{0,1},{1,2},{2,3},{3,4},{4,5},{5,6},{6,7},{7,8},{8,9},{9,10},{10,1... | collective-permute-start | bytes 6536 | tf_op jit(solution)/shard_map/ppermute | solution.py:22
  69.9 33.4 %collective-permute-start.6 = (f32[8,2,34,1]{3,0,2,1:T(8,128)S(1)}, f32[8,2,34,1]{3,0,2,1:T(8,128)S(1)}, u32[]{:S(2)}, u32[]{:S(2)}) collective-permute-start(f32[8,2,34,1]{3,0,2,1:T(8,128)S(1)} %get-tuple-element.29), channel_id=1, source_target_pairs={{1,0},{2,1},{3,2},{4,3},{5,4},{6,5},{7,6},{8,7},{9,8},{10,9},{11,1... | collective-permute-start | bytes 6536 | tf_op jit(solution)/shard_map/ppermute | solution.py:24
  104.8 5.6 collective-permute-start.8
  107.3 4.9 collective-permute-start.9
  112.4 26.0 %collective-permute-start.11 = (f32[8,2,34,1]{3,0,2,1:T(8,128)S(1)}, f32[8,2,34,1]{3,0,2,1:T(8,128)S(1)}, u32[]{:S(2)}, u32[]{:S(2)}) collective-permute-start(f32[8,2,34,1]{3,0,2,1:T(8,128)S(1)} %get-tuple-element.26), channel_id=1, source_target_pairs={{0,1},{1,2},{2,3},{3,4},{4,5},{5,6},{6,7},{7,8},{8,9},{9,10},{10,1... | collective-permute-start | bytes 6536 | tf_op jit(solution)/shard_map/ppermute | solution.py:22
  114.3 24.0 %collective-permute-start.10 = (f32[8,2,34,1]{3,0,2,1:T(8,128)S(1)}, f32[8,2,34,1]{3,0,2,1:T(8,128)S(1)}, u32[]{:S(2)}, u32[]{:S(2)}) collective-permute-start(f32[8,2,34,1]{3,0,2,1:T(8,128)S(1)} %get-tuple-element.27), channel_id=1, source_target_pairs={{1,0},{2,1},{3,2},{4,3},{5,4},{6,5},{7,6},{8,7},{9,8},{10,9},{11,1... | collective-permute-start | bytes 6536 | tf_op jit(solution)/shard_map/ppermute | solution.py:24
  138.9 8.5 collective-permute-start.12
  148.4 20.0 %collective-permute-start.14 = (f32[8,2,34,1]{3,0,2,1:T(8,128)S(1)}, f32[8,2,34,1]{3,0,2,1:T(8,128)S(1)}, u32[]{:S(2)}, u32[]{:S(2)}) collective-permute-start(f32[8,2,34,1]{3,0,2,1:T(8,128)S(1)} %get-tuple-element.25), channel_id=1, source_target_pairs={{1,0},{2,1},{3,2},{4,3},{5,4},{6,5},{7,6},{8,7},{9,8},{10,9},{11,1... | collective-permute-start | bytes 6536 | tf_op jit(solution)/shard_map/ppermute | solution.py:24
  158.3 26.2 %collective-permute-start.15 = (f32[8,2,34,1]{3,0,2,1:T(8,128)S(1)}, f32[8,2,34,1]{3,0,2,1:T(8,128)S(1)}, u32[]{:S(2)}, u32[]{:S(2)}) collective-permute-start(f32[8,2,34,1]{3,0,2,1:T(8,128)S(1)} %get-tuple-element.24), channel_id=1, source_target_pairs={{0,1},{1,2},{2,3},{3,4},{4,5},{5,6},{6,7},{7,8},{8,9},{9,10},{10,1... | collective-permute-start | bytes 6536 | tf_op jit(solution)/shard_map/ppermute | solution.py:22
  185.1 7.9 collective-permute-start.16
  188.1 5.7 collective-permute-start.17
  194.0 18.5 %collective-permute-start.19 = (f32[8,2,34,1]{3,0,2,1:T(8,128)S(1)}, f32[8,2,34,1]{3,0,2,1:T(8,128)S(1)}, u32[]{:S(2)}, u32[]{:S(2)}) collective-permute-start(f32[8,2,34,1]{3,0,2,1:T(8,128)S(1)} %get-tuple-element.22), channel_id=1, source_target_pairs={{0,1},{1,2},{2,3},{3,4},{4,5},{5,6},{6,7},{7,8},{8,9},{9,10},{10,1... | collective-permute-start | bytes 6536 | tf_op jit(solution)/shard_map/ppermute | solution.py:22
  195.9 16.6 %collective-permute-start.18 = (f32[8,2,34,1]{3,0,2,1:T(8,128)S(1)}, f32[8,2,34,1]{3,0,2,1:T(8,128)S(1)}, u32[]{:S(2)}, u32[]{:S(2)}) collective-permute-start(f32[8,2,34,1]{3,0,2,1:T(8,128)S(1)} %get-tuple-element.23), channel_id=1, source_target_pairs={{1,0},{2,1},{3,2},{4,3},{5,4},{6,5},{7,6},{8,7},{9,8},{10,9},{11,1... | collective-permute-start | bytes 6536 | tf_op jit(solution)/shard_map/ppermute | solution.py:24
  212.9 8.4 collective-permute-start.20
  222.2 19.6 %collective-permute-start.23 = (f32[8,2,34,1]{3,0,2,1:T(8,128)S(1)}, f32[8,2,34,1]{3,0,2,1:T(8,128)S(1)}, u32[]{:S(2)}, u32[]{:S(2)}) collective-permute-start(f32[8,2,34,1]{3,0,2,1:T(8,128)S(1)} %get-tuple-element.20), channel_id=1, source_target_pairs={{0,1},{1,2},{2,3},{3,4},{4,5},{5,6},{6,7},{7,8},{8,9},{9,10},{10,1... | collective-permute-start | bytes 6536 | tf_op jit(solution)/shard_map/ppermute | solution.py:22
  224.2 17.7 %collective-permute-start.22 = (f32[8,2,34,1]{3,0,2,1:T(8,128)S(1)}, f32[8,2,34,1]{3,0,2,1:T(8,128)S(1)}, u32[]{:S(2)}, u32[]{:S(2)}) collective-permute-start(f32[8,2,34,1]{3,0,2,1:T(8,128)S(1)} %get-tuple-element.21), channel_id=1, source_target_pairs={{1,0},{2,1},{3,2},{4,3},{5,4},{6,5},{7,6},{8,7},{9,8},{10,9},{11,1... | collective-permute-start | bytes 6536 | tf_op jit(solution)/shard_map/ppermute | solution.py:24
  242.3 6.4 collective-permute-start.24
  250.0 23.8 %collective-permute-start.27 = (f32[8,2,34,1]{3,0,2,1:T(8,128)S(1)}, f32[8,2,34,1]{3,0,2,1:T(8,128)S(1)}, u32[]{:S(2)}, u32[]{:S(2)}) collective-permute-start(f32[8,2,34,1]{3,0,2,1:T(8,128)S(1)} %get-tuple-element.18), channel_id=1, source_target_pairs={{0,1},{1,2},{2,3},{3,4},{4,5},{5,6},{6,7},{7,8},{8,9},{9,10},{10,1... | collective-permute-start | bytes 6536 | tf_op jit(solution)/shard_map/ppermute | solution.py:22
  252.0 21.9 %collective-permute-start.26 = (f32[8,2,34,1]{3,0,2,1:T(8,128)S(1)}, f32[8,2,34,1]{3,0,2,1:T(8,128)S(1)}, u32[]{:S(2)}, u32[]{:S(2)}) collective-permute-start(f32[8,2,34,1]{3,0,2,1:T(8,128)S(1)} %get-tuple-element.19), channel_id=1, source_target_pairs={{1,0},{2,1},{3,2},{4,3},{5,4},{6,5},{7,6},{8,7},{9,8},{10,9},{11,1... | collective-permute-start | bytes 6536 | tf_op jit(solution)/shard_map/ppermute | solution.py:24
  274.3 5.8 collective-permute-start.28
  278.2 14.0 %collective-permute-start.29 = (f32[8,2,1,64]{3,0,2,1:T(8,128)S(1)}, f32[8,2,1,64]{3,0,2,1:T(8,128)S(1)}, u32[]{:S(2)}, u32[]{:S(2)}) collective-permute-start(f32[8,2,1,64]{3,0,2,1:T(8,128)S(1)} %get-tuple-element.32), channel_id=1, source_target_pairs={{0,16},{16,32},{32,48},{48,64},{64,80},{80,96},{96,112},{112,128},... | collective-permute-start | bytes 12296 | tf_op jit(solution)/shard_map/ppermute | solution.py:22
  292.3 13.8 %collective-permute-start.30 = (f32[8,2,34,1]{3,0,2,1:T(8,128)S(1)}, f32[8,2,34,1]{3,0,2,1:T(8,128)S(1)}, u32[]{:S(2)}, u32[]{:S(2)}) collective-permute-start(f32[8,2,34,1]{3,0,2,1:T(8,128)S(1)} %get-tuple-element.17), channel_id=1, source_target_pairs={{1,0},{2,1},{3,2},{4,3},{5,4},{6,5},{7,6},{8,7},{9,8},{10,9},{11,1... | collective-permute-start | bytes 6536 | tf_op jit(solution)/shard_map/ppermute | solution.py:24
  302.4 13.3 %collective-permute-start.31 = (f32[8,2,34,1]{3,0,2,1:T(8,128)S(1)}, f32[8,2,34,1]{3,0,2,1:T(8,128)S(1)}, u32[]{:S(2)}, u32[]{:S(2)}) collective-permute-start(f32[8,2,34,1]{3,0,2,1:T(8,128)S(1)} %get-tuple-element.16), channel_id=1, source_target_pairs={{0,1},{1,2},{2,3},{3,4},{4,5},{5,6},{6,7},{7,8},{8,9},{9,10},{10,1... | collective-permute-start | bytes 6536 | tf_op jit(solution)/shard_map/ppermute | solution.py:22
  318.3 474.5 %all-gather.2.cloned.1.call-start = ((), (), s32[]{:S(2)}) async-start(), calls=%async_computation.3 | async-start | bytes 8650752 | tf_op jit(solution)/shard_map/all_gather | solution.py:67
  319.1 537.7 %reduce-scatter.9.cloned.1.call-start = ((), (), s32[]{:S(2)}) async-start(), calls=%async_computation.5 | async-start | bytes 540672 | tf_op jit(solution)/shard_map/reduce_scatter | solution.py:87
  714.7 256.3 %reduce-scatter.11.cloned.1.call-start = ((), (), s32[]{:S(2)}) async-start(), calls=%async_computation.6 | async-start | bytes 557056
  (11 other events, 1428.9 us)
Sparse Core Ops, SparseCore 0:
  318.4 175.8 reduce-scatter.6
  496.7 193.0 all-gather.1
  714.8 141.9 reduce-scatter.8
  860.7 110.2 reduce-scatter.10
where the time goes:
time: 981 us; the launch traced here: 979 us
  waiting for transfers between devices  481 us (49%)
  blocking collectives  289 us (29%)
  starting transfers between devices  155 us (16%)
  matrix products  25.9 us (3%)
  between operations  15.2 us (2%)
    all_gather x1, blocking collectives, shards(): lax.all_gather(projected, ('grp', 'gz'), axis=3, tiled=True)  212 us
    reduce_scatter x1, waiting for transfers between devices, shards(): lax.psum_scatter(partial_proj, 'sim', scatter_dimension=2, tiled=True)  173 us
    ppermute x16, starting transfers between devices, with_halo(): lax.ppermute(head, axis, [((i + 1) % count, i) for i in range(count)])  114 us
    unnamed x5, waiting for transfers between devices  114 us
    ppermute x16, waiting for transfers between devices, with_halo(): lax.ppermute(tail, axis, [(i, (i + 1) % count) for i in range(count)])  92.5 us
    unnamed x1, blocking collectives  77.3 us
    reduce_scatter x1, waiting for transfers between devices, shards(): lax.psum_scatter(block, 'sim', scatter_dimension=1, tiled=True)  52.4 us
    ppermute x16, waiting for transfers between devices, with_halo(): lax.ppermute(head, axis, [((i + 1) % count, i) for i in range(count)])  49.3 us
  transfers between devices with their start and end apart: 36, of which 22 were waited for; matrix products, arithmetic and copies ran while one was open for 3% of the time, Pallas kernels for 0%

commit v1 on v0

v1 whole, which is shorter than its diff:
```python
import functools

import jax
import jax.numpy as jnp
from jax import lax
from jax.experimental import pallas as pl
from jax.experimental.pallas import tpu as pltpu
from jax.sharding import PartitionSpec as P

NF = 8
NX = 1024
NY = 1024
RANK = 128
NZ = 2
STEPS = 2
Q = 4
XR = 32
YC = 64
HALO = 8
ROWS = XR + 2 * HALO
LANES = 128
HF = NF // 2
MESH = pl.DeviceIdType.MESH
F32 = jnp.float32
BF16 = jnp.bfloat16


def split(a):
    hi = a.astype(BF16)
    lo = (a - hi.astype(F32)).astype(BF16)
    return hi, lo


def dot(a, b, dims):
    return lax.dot_general(a, b, (dims, ((), ())), preferred_element_type=F32)


def dot3(a, b, dims):
    ah, al = split(a)
    bh, bl = split(b)
    return dot(ah, bh, dims) + (dot(ah, bl, dims) + dot(al, bh, dims))


NN = ((1,), (0,))
NT = ((1,), (1,))


def kernel(
    u_ref, diff_ref, vel_ref, coup_ref, bx_ref, by_ref,
    uo_ref, gx_ref, gy_ref, core_ref,
    w, el, er, hl, hr, v, base, acc, th,
    a_ref, gyb, gzb, ct, ra, pbx, rb, pf, rp, pd, gh, gxb, ds, rd, pby, rdb, cot, rc, et, bxt, byt,
    s_halo, r_halo, s_yc, r_yc, s_zc, r_zc, s_pz, r_pz, s_zh, r_zh, s_px, r_px,
    s_ra, r_ra, s_rb, r_rb, s_rd, r_rd, s_rdb, r_rdb, s_co, r_co,
):
    sim = lax.axis_index("sim")
    zh = lax.axis_index("grp")
    x = lax.axis_index("gz")
    zl = sim // (2 * Q)
    y = (sim // 2) % Q
    c = sim % 2
    nsim = 2 * Q * Q
    nblk = Q * Q
    blk = zh * Q + x

    def dev(zl_, y_, c_, zh_, x_):
        return (zl_ * (2 * Q) + y_ * 2 + c_, zh_, x_)

    def cyc(i, d):
        return (i + d + Q) % Q

    def halo_dev(dx, dy):
        b = (blk + dy + nblk) % nblk
        return ((sim + dx + nsim) % nsim, b // Q, b % Q)

    pairs = [(d, e) for d in range(Q) for e in range(2) if (d, e) != (0, 0)]
    self_b = zl == zh
    self_d = (x == y) & (c == zl // 2)

    barrier = pltpu.get_barrier_semaphore()

    def tell(d):
        pl.semaphore_signal(barrier, inc=1, device_id=d, device_id_type=MESH)

    halo_dirs = [(dx, dy) for dx in (-1, 0, 1) for dy in (-1, 0, 1) if (dx, dy) != (0, 0)]
    for dx, dy in halo_dirs:
        tell(halo_dev(dx, dy))
    for d, e in pairs:
        tell(dev(zl, cyc(y, -d), c ^ e, zh, x))
        tell(dev(zl, y, c ^ e, zh, cyc(x, -d)))
        if d:
            tell(dev(cyc(zl, -d), y, c ^ e, zh, x))
    for d in range(1, Q):
        tell(dev(zl, y, c, cyc(zh, -d), x))
    for k in range(Q):
        @pl.when(~(self_b & (k == zh)))
        def _():
            tell(dev(zh, y, c, k, x))

        @pl.when(~(self_d & (k == zl)))
        def _():
            tell(dev(k, x, zl // 2, zh, y))

    sends = []

    def send(src, dst, ssem, rsem, target):
        copy = pltpu.make_async_remote_copy(
            src_ref=src, dst_ref=dst, send_sem=ssem, recv_sem=rsem, device_id=target, device_id_type=MESH
        )
        copy.start()
        sends.append(copy)

    def arrive(dst, ssem, rsem, source):
        pltpu.make_async_remote_copy(
            src_ref=dst, dst_ref=dst, send_sem=ssem, recv_sem=rsem, device_id=source, device_id_type=MESH
        ).wait_recv()

    def lane(shape):
        return lax.broadcasted_iota(jnp.int32, shape, len(shape) - 1)

    zero = jnp.zeros((XR, LANES), F32)
    lane32 = lane((XR, LANES))
    left = zero
    right = zero
    for fz in range(NF * NZ):
        w[fz, 0:XR, :] = zero
        w[fz, 0:XR, 0:YC] = u_ref[fz // NZ, fz % NZ]
    for fz in range(NF * NZ):
        own = w[fz, 0:XR, :]
        here = lane32 // HALO == fz
        left = jnp.where(here, pltpu.roll(own, fz * HALO, 1) if fz else own, left)
        right = jnp.where(here, pltpu.roll(own, (fz * HALO - (YC - HALO)) % LANES, 1) if fz != 7 else own, right)
    el[...] = left
    er[...] = right

    out_count = jnp.int32(8 + 7 + 6 + 3 + 7 + 2 * Q) - self_b.astype(jnp.int32) - self_d.astype(jnp.int32)
    pl.semaphore_wait(barrier, out_count)

    def halo_sem(dx, dy):
        return (dx + 1) * 3 + dy + 1

    top, bottom = pl.ds(0, HALO), pl.ds(XR - HALO, HALO)
    below, above, mine = pl.ds(XR, HALO), pl.ds(XR + HALO, HALO), pl.ds(0, XR)
    halo_plan = [
        (-1, 0, w.at[:, top], w.at[:, below]),
        (1, 0, w.at[:, bottom], w.at[:, above]),
        (0, -1, el, hr.at[mine]),
        (0, 1, er, hl.at[mine]),
        (-1, -1, el.at[top], hr.at[below]),
        (1, -1, el.at[bottom], hr.at[above]),
        (-1, 1, er.at[top], hl.at[below]),
        (1, 1, er.at[bottom], hl.at[above]),
    ]
    for dx, dy, src, dst in halo_plan:
        i = halo_sem(dx, dy)
        send(src, dst, s_halo.at[i], r_halo.at[i], halo_dev(dx, dy))

    bxt[...] = bx_ref[pl.ds(pl.multiple_of(zl * 256, 256), 256), :].astype(F32).T.astype(BF16)
    byt[...] = jnp.concatenate(
        [by_ref[pl.ds(pl.multiple_of((k * Q + x) * YC, YC), YC), :].astype(F32) for k in range(Q)], axis=0
    ).T.astype(BF16)

    for dx, dy, src, dst in halo_plan:
        i = halo_sem(dx, dy)
        arrive(dst, s_halo.at[i], r_halo.at[i], halo_dev(-dx, -dy))

    lane48 = lane((ROWS, LANES))
    is_right = (lane48 >= YC) & (lane48 < YC + HALO)
    is_left = lane48 >= LANES - HALO
    for fz in range(NF * NZ):
        from_left = pltpu.roll(hl[...], (LANES - HALO - fz * HALO) % LANES, 1) if fz != 15 else hl[...]
        from_right = pltpu.roll(hr[...], (YC - fz * HALO) % LANES, 1) if fz != 8 else hr[...]
        full = jnp.where(is_left, from_left, jnp.where(is_right, from_right, w[fz]))
        v[fz // NZ, fz % NZ] = full
        base[fz // NZ, fz % NZ] = full
        th[0, fz // NZ, fz % NZ] = jnp.tanh(full)

    def step(_, carry):
        for stage in range(4):
            now, later = stage % 2, (stage + 1) % 2

            def field(f, carry2):
                d = diff_ref[f]
                vx = vel_ref[0, f] * 0.5
                vy = vel_ref[1, f] * 0.5
                for z in range(NZ):
                    s = v[f, z]
                    k = th[now, 0, z] * coup_ref[f, 0]
                    for g in range(1, NF):
                        k = k + th[now, g, z] * coup_ref[f, g]
                    k = k + s * (-6.0 * d) + pltpu.roll(s, ROWS - 1, 0) * (d - vx) + pltpu.roll(s, 1, 0) * (d + vx)
                    k = k + pltpu.roll(s, LANES - 1, 1) * (d - vy) + pltpu.roll(s, 1, 1) * (d + vy)
                    if z == 0:
                        first = k + v[f, 1] * (2.0 * d)
                        s0 = s
                    else:
                        second = k + s0 * (2.0 * d)
                for z, k in ((0, first), (1, second)):
                    if stage == 0:
                        acc[f, z] = k
                        new = base[f, z] + 0.5 * k
                    elif stage == 1:
                        acc[f, z] = acc[f, z] + 2.0 * k
                        new = base[f, z] + 0.5 * k
                    elif stage == 2:
                        acc[f, z] = acc[f, z] + 2.0 * k
                        new = base[f, z] + k
                    else:
                        new = base[f, z] + (acc[f, z] + k) * (1.0 / 6.0)
                        base[f, z] = new
                    v[f, z] = new
                    th[later, f, z] = jnp.tanh(new)
                return carry2

            lax.fori_loop(0, NF, field, 0)
        return carry

    lax.fori_loop(0, STEPS, step, 0)

    low32 = lane32 < YC
    for f in range(NF):
        a_ref[f] = jnp.where(low32, base[f, 0, 0:XR, :], pltpu.roll(base[f, 1, 0:XR, :], YC, 1))

    me_yc = y * 2 + c
    me_zc = c * Q + zl
    for d, e in pairs:
        ty, tc = cyc(y, d), c ^ e
        send(a_ref.at[pl.ds(tc * HF, HF)], gyb.at[me_yc], s_yc.at[d * 2 + e], r_yc.at[me_yc], dev(zl, ty, tc, zh, x))
    for d, e in pairs:
        if d:
            tz, tc = cyc(zl, d), c ^ e
            send(a_ref.at[pl.ds(tc * HF, HF)], gzb.at[me_zc], s_zc.at[d * 2 + e], r_zc.at[me_zc], dev(tz, y, tc, zh, x))
    for f in range(NF):
        for z in range(NZ):
            uo_ref[f, z] = base[f, z, 0:XR, 0:YC]
    gyb[me_yc] = a_ref[pl.ds(c * HF, HF)]

    for d, e in pairs:
        sy, sc = cyc(y, -d), c ^ e
        i = sy * 2 + sc
        arrive(gyb.at[i], s_yc.at[d * 2 + e], r_yc.at[i], dev(zl, sy, sc, zh, x))

    def wide(ref):
        return jnp.concatenate([ref[:, f].reshape(2 * Q * XR, LANES) for f in range(HF)], axis=1)

    gyw = wide(gyb)
    gyh, gyl = split(gyw)
    part = dot(bxt[...], gyh, NN) + dot(bxt[...], gyl, NN)
    for f in range(HF):
        pf[f] = part[:, f * LANES:(f + 1) * LANES]

    def rank_rows(z_):
        return pl.ds(pl.multiple_of(z_ * 32 + y * 8, 8), 8)

    for d in range(1, Q):
        tz = cyc(zl, d)
        send(pf.at[:, rank_rows(tz)], rp.at[zl], s_pz.at[d], r_pz.at[zl], dev(tz, y, c, zh, x))
    rp[zl] = pf[:, rank_rows(zl), :]
    for e in range(2):
        gzb[e * Q + zl] = gyb[y * 2 + e]

    for d, e in pairs:
        if d:
            sz, sc = cyc(zl, -d), c ^ e
            i = sc * Q + sz
            arrive(gzb.at[i], s_zc.at[d * 2 + e], r_zc.at[i], dev(sz, y, sc, zh, x))
    gzh, gzl = split(wide(gzb))
    block = dot(gyh, gzh, NT) + (dot(gyh, gzl, NT) + dot(gyl, gzh, NT))
    for k in range(Q):
        for e in range(2):
            ct[k, e] = block[k * YC:(k + 1) * YC, e * LANES:(e + 1) * LANES]
    me_xc = x * 2 + c
    for d, e in pairs:
        tx, tc = cyc(x, d), c ^ e
        send(ct.at[tx, tc], ra.at[me_xc], s_ra.at[d * 2 + e], r_ra.at[me_xc], dev(zl, y, tc, zh, tx))
    ra[me_xc] = ct[x, c]

    for d in range(1, Q):
        sz = cyc(zl, -d)
        arrive(rp.at[sz], s_pz.at[d], r_pz.at[sz], dev(sz, y, c, zh, x))
    own = (rp[0] + rp[1]) + (rp[2] + rp[3])
    pd[...] = own
    for d in range(1, Q):
        th_ = cyc(zh, d)
        send(pd, gh.at[zh], s_zh.at[d], r_zh.at[zh], dev(zl, y, c, th_, x))
    for d in range(1, Q):
        tx = cyc(x, d)
        send(pd, gxb.at[x], s_px.at[d], r_px.at[x], dev(zl, y, c, zh, tx))
    gh[zh] = own
    gxb[x] = own

    for d, e in pairs:
        sx, sc = cyc(x, -d), c ^ e
        i = sx * 2 + sc
        arrive(ra.at[i], s_ra.at[d * 2 + e], r_ra.at[i], dev(zl, y, sc, zh, sx))
    total = ra[0]
    for i in range(1, 2 * Q):
        total = total + ra[i]
    turned = jnp.concatenate([total, total], axis=0).T
    low16 = lane((16, LANES)) < YC
    late = []
    for k in range(Q):
        pbx[k] = jnp.where(low16, turned[k * 32:k * 32 + 16], turned[k * 32 + 16:k * 32 + 32])
        same = self_b & (k == zl)
        copy = pltpu.make_async_remote_copy(
            src_ref=pbx.at[k], dst_ref=rb.at[zh], send_sem=s_rb.at[k], recv_sem=r_rb.at[zh],
            device_id=dev(k, y, c, zl, x), device_id_type=MESH,
        )
        late.append((same, copy))

        @pl.when(same)
        def _():
            rb[zh] = pbx[k]

        @pl.when(~same)
        def _():
            copy.start()

    for d in range(1, Q):
        sh = cyc(zh, -d)
        arrive(gh.at[sh], s_zh.at[d], r_zh.at[sh], dev(zl, y, c, sh, x))
    low = lane((32, LANES)) < YC

    def unpack(ref):
        g = [ref[k].reshape(32, LANES) for k in range(Q)]
        r = [pltpu.roll(t, YC, 1) for t in g]
        first = jnp.concatenate([jnp.where(low, g[0], r[1]), jnp.where(low, g[2], r[3])], axis=1)
        second = jnp.concatenate([jnp.where(low, r[0], g[1]), jnp.where(low, r[2], g[3])], axis=1)
        return jnp.concatenate([first, second], axis=0)

    cols = unpack(gh)
    ch, cl = split(cols)
    two_h = jnp.concatenate([ch, ch], axis=0)
    two_l = jnp.concatenate([cl, cl], axis=0)
    cot[...] = dot(byt[...], two_h, NT) + dot(byt[...], two_l, NT)

    def core_rows(x_):
        return pl.ds(pl.multiple_of(zh * 32 + x_ * 8, 8), 8)

    for d, e in pairs:
        tx, tc = cyc(x, d), c ^ e
        send(cot.at[core_rows(tx)], rc.at[me_xc], s_co.at[d * 2 + e], r_co.at[me_xc], dev(zl, y, tc, zh, tx))
    rc[me_xc] = cot[core_rows(x), :]

    for d in range(1, Q):
        sx = cyc(x, -d)
        arrive(gxb.at[sx], s_px.at[d], r_px.at[sx], dev(zl, y, c, zh, sx))
    rh, rl = split(unpack(gxb).T)
    dd = dot(rh, ch, NN) + (dot(rh, cl, NN) + dot(rl, ch, NN))
    for k in range(Q):
        for e in range(2):
            ds[k, e] = dd[k * YC:(k + 1) * YC, e * LANES:(e + 1) * LANES]
    for d, e in pairs:
        ty, tc = cyc(y, d), c ^ e
        send(ds.at[ty, tc], rd.at[me_yc], s_rd.at[d * 2 + e], r_rd.at[me_yc], dev(zl, ty, tc, zh, x))
    rd[me_yc] = ds[y, c]

    for k in range(Q):
        @pl.when(~(self_b & (k == zh)))
        def _():
            arrive(rb.at[k], s_rb.at[k], r_rb.at[k], dev(zh, y, c, k, x))
    gsum = ((rb[0] + rb[1]) + (rb[2] + rb[3])) * (1.0 / (NF * NZ * NY))
    gx_ref[0:16, :] = gsum[:, 0:YC]
    gx_ref[16:32, :] = pltpu.roll(gsum, YC, 1)[:, 0:YC]

    for d, e in pairs:
        sy, sc = cyc(y, -d), c ^ e
        i = sy * 2 + sc
        arrive(rd.at[i], s_rd.at[d * 2 + e], r_rd.at[i], dev(zl, sy, sc, zh, x))
    total = rd[0]
    for i in range(1, 2 * Q):
        total = total + rd[i]
    lane16 = lane((16, LANES))
    for k in range(2):
        for h in range(2):
            packed = jnp.zeros((16, LANES), F32)
            for j in range(4):
                piece = total[j * 16:(j + 1) * 16]
                shift = (j * 32 - k * 64 - h * 32) % LANES
                piece = pltpu.roll(piece, shift, 1) if shift else piece
                packed = jnp.where(lane16 // 32 == j, piece, packed)
            m = k * 2 + h
            pby[m] = packed
            same = self_d & (2 * c + k == zl) & (c == h)
            copy = pltpu.make_async_remote_copy(
                src_ref=pby.at[m], dst_ref=rdb.at[zl], send_sem=s_rdb.at[m], recv_sem=r_rdb.at[zl],
                device_id=dev(2 * c + k, x, h, zh, y), device_id_type=MESH,
            )
            late.append((same, copy))

            @pl.when(same)
            def _():
                rdb[zl] = pby[m]

            @pl.when(~same)
            def _():
                copy.start()

    for d, e in pairs:
        sx, sc = cyc(x, -d), c ^ e
        i = sx * 2 + sc
        arrive(rc.at[i], s_co.at[d * 2 + e], r_co.at[i], dev(zl, y, sc, zh, sx))
    e0 = (rc[0] + rc[2]) + (rc[4] + rc[6])
    e1 = (rc[1] + rc[3]) + (rc[5] + rc[7])
    both = jnp.where(lane((8, LANES)) < 64, e0, e1)
    et[...] = jnp.concatenate([both] * 16, axis=0).T
    for fh in range(2):
        for z in range(NZ):
            for f in range(HF):
                at = fh * 64 + z * 32 + f * 8
                core_ref[fh * HF + f, z] = jnp.where(c == 0, et[at:at + 4, 0:8], et[at + 4:at + 8, 0:8])

    for k in range(Q):
        @pl.when(~(self_d & (k == zl)))
        def _():
            arrive(rdb.at[k], s_rdb.at[k], r_rdb.at[k], dev(k, x, zl // 2, zh, y))
    gsum = ((rdb[0] + rdb[1]) + (rdb[2] + rdb[3])) * (1.0 / (NF * NZ * RANK))
    for j in range(4):
        gy_ref[j * 16:(j + 1) * 16, :] = (pltpu.roll(gsum, LANES - j * 32, 1) if j else gsum)[:, 0:32]

    for copy in sends:
        copy.wait_send()
    for same, copy in late:
        @pl.when(~same)
        def _():
            copy.wait_send()


def shards(fields, diffusivity, velocity, coupling, basis_x, basis_y):
    vm = lambda *shape: pltpu.VMEM(shape, F32)
    dma = lambda n: pltpu.SemaphoreType.DMA((n,))
    vspec = pl.BlockSpec(memory_space=pltpu.VMEM)
    sspec = pl.BlockSpec(memory_space=pltpu.SMEM)
    scratch = [
        vm(NF * NZ, ROWS, LANES), vm(XR, LANES), vm(XR, LANES), vm(ROWS, LANES), vm(ROWS, LANES),
        vm(NF, NZ, ROWS, LANES), vm(NF, NZ, ROWS, LANES), vm(NF, NZ, ROWS, LANES), vm(2, NF, NZ, ROWS, LANES),
        vm(NF, XR, LANES),
        vm(2 * Q, HF, XR, LANES), vm(2 * Q, HF, XR, LANES),
        vm(Q, 2, YC, LANES), vm(2 * Q, YC, LANES), vm(Q, 16, LANES), vm(Q, 16, LANES),
        vm(HF, RANK, LANES), vm(Q, HF, 8, LANES), vm(HF, 8, LANES),
        vm(Q, HF, 8, LANES), vm(Q, HF, 8, LANES),
        vm(Q, 2, YC, LANES), vm(2 * Q, YC, LANES), vm(Q, 16, LANES), vm(Q, 16, LANES),
        vm(RANK, LANES), vm(2 * Q, 8, LANES), vm(LANES, LANES),
        pltpu.VMEM((RANK, 256), BF16), pltpu.VMEM((RANK, 256), BF16),
        dma(9), dma(9), dma(8), dma(8), dma(8), dma(8), dma(4), dma(4), dma(4), dma(4), dma(4), dma(4),
        dma(8), dma(8), dma(4), dma(4), dma(8), dma(8), dma(4), dma(4), dma(8), dma(8),
    ]
    return pl.pallas_call(
        kernel,
        out_shape=(
            jax.ShapeDtypeStruct((NF, NZ, XR, YC), F32),
            jax.ShapeDtypeStruct((XR, YC), F32),
            jax.ShapeDtypeStruct((YC, XR), F32),
            jax.ShapeDtypeStruct((NF, NZ, 4, 8), F32),
        ),
        in_specs=[vspec, sspec, sspec, sspec, vspec, vspec],
        out_specs=(vspec, vspec, vspec, vspec),
        scratch_shapes=scratch,
        compiler_params=pltpu.CompilerParams(
            collective_id=0, has_side_effects=True, vmem_limit_bytes=40 * 1024 * 1024
        ),
    )(fields, diffusivity, velocity, coupling, basis_x, basis_y)


def solution(mesh):
    in_specs = (P(None, None, "sim", ("grp", "gz")), P(), P(), P(), P(), P())
    out_specs = (
        P(None, None, "sim", ("grp", "gz")),
        P("sim", ("grp", "gz")),
        P(("grp", "gz"), "sim"),
        P(None, None, "sim", ("grp", "gz")),
    )
    return jax.shard_map(shards, mesh=mesh, in_specs=in_specs, out_specs=out_specs, check_vma=False)
```

time: 981 us -> 73.9 us (0.08)
  waiting for transfers between devices: 481 us -> 0 us
  blocking collectives: 289 us -> 0 us
  starting transfers between devices: 155 us -> 0 us
  Pallas kernels: 0 us -> 65.5 us
  matrix products: 25.9 us -> 0 us
  between operations: 15.2 us -> 0.66 us
    reduce_scatter x2 -> x0, waiting for transfers between devices: 226 us -> none  [the longest x1 173 us: shards(): lax.psum_scatter(partial_proj, 'sim', scatter_dimension=2, tiled=True)]
    all_gather x1 -> x0, blocking collectives: 212 us -> none  [shards(): lax.all_gather(projected, ('grp', 'gz'), axis=3, tiled=True)]
    ppermute x32 -> x0, starting transfers between devices: 155 us -> none  [the longest x16 114 us: with_halo(): lax.ppermute(head, axis, [((i + 1) % count, i) for i in range(count)])]
    ppermute x32 -> x0, waiting for transfers between devices: 142 us -> none  [the longest x16 92.5 us: with_halo(): lax.ppermute(tail, axis, [(i, (i + 1) % count) for i in range(count)])]
    unnamed x5 -> x0, waiting for transfers between devices: 114 us -> none
    unnamed x1 -> x0, blocking collectives: 77.3 us -> none
    pallas_call x0 -> x1, Pallas kernels: none -> 65.5 us  [shards(): pl.pallas_call(kernel, out_shape=(jax.ShapeDtypeStruct((NF, NZ, XR, YC),...]
    dot_general x12 -> x0, matrix products: 25.9 us -> none  [the longest x1 10.7 us: shards(): jnp.einsum('fzxy,fzwy->xw', state, lax.all_gather(state, 'sim', axis=2, t...]
  transfers between devices with their start and end apart: 36 -> 0, of which waited for: 22 -> 0; matrix products, arithmetic and copies ran while one was open for 3% -> 0% of each run, Pallas kernels for 0% -> 0%
where the time goes in v1:
time: 73.9 us; the launch traced here: 73.7 us
  Pallas kernels  65.5 us (89%)
  local copies, waits for them, and re-layouts  7.46 us (10%)
    pallas_call x1, Pallas kernels, shards(): pl.pallas_call(kernel, out_shape=(jax.ShapeDtypeStruct((NF, NZ, XR, YC),...  65.5 us
    unnamed x15, local copies, waits for them, and re-layouts  6.78 us

profile of v1, /device:TPU:1, one launch (start us, length us, event | category | flops | bytes accessed | tf_op | source)
XLA Modules:
  0.0 73.7 jit_solution(21876694823085182)
XLA Ops:
  0.6 0.0 copy-start
  0.6 0.9 %copy-done = f32[8,2,32,64]{3,2,1,0:T(8,128)S(1)} copy-done((f32[8,2,32,64]{3,2,1,0:T(8,128)S(1)}, f32[8,2,32,64]{3,2,1,0:T(8,128)}, u32[]{:S(2)}) %copy-start) | copy-done | bytes 131096
  1.6 0.0 copy-start.1
  1.6 0.9 %copy-done.1 = bf16[1024,128]{1,0:T(8,128)(2,1)S(1)} copy-done((bf16[1024,128]{1,0:T(8,128)(2,1)S(1)}, bf16[1024,128]{1,0:T(8,128)(2,1)}, u32[]{:S(2)}) %copy-start.1) | copy-done | bytes 262168
  2.5 0.0 copy-start.2
  2.5 0.9 %copy-done.2 = bf16[1024,128]{1,0:T(8,128)(2,1)S(1)} copy-done((bf16[1024,128]{1,0:T(8,128)(2,1)S(1)}, bf16[1024,128]{1,0:T(8,128)(2,1)}, u32[]{:S(2)}) %copy-start.2) | copy-done | bytes 262168
  3.5 0.0 copy-start.3
  3.5 0.7 copy-done.3
  4.2 0.0 copy-start.4
  4.2 0.7 copy-done.4
  4.9 0.0 copy-start.5
  4.9 0.7 copy-done.5
  5.5 65.5 %shard_map.93 = (f32[8,2,32,64]{3,2,1,0:T(8,128)S(1)}, f32[32,64]{1,0:T(8,128)S(1)}, f32[64,32]{1,0:T(8,128)S(1)}, f32[8,2,4,8]{3,2,1,0:T(4,128)S(1)}) custom-call(f32[8,2,32,64]{3,2,1,0:T(8,128)S(1)} %copy-done, f32[8]{0:T(128)S(1)} %copy-done.5, f32[2,8]{1,0:T(2,128)S(1)} %copy-done.4, f32[8,8]{1,0:T(8,128)S(1)} %copy-done.3, ...), custom_call_target="tpu_custom_call" | custom-call | tf_op jit(solution)/shard_map/pallas_call | solution.py:448
  71.1 0.7 copy.10
  71.7 0.7 copy.14
  72.4 0.6 copy.15
  73.0 0.6 copy.16
Async XLA Ops:
  0.6 1.0 %copy-start = (f32[8,2,32,64]{3,2,1,0:T(8,128)S(1)}, f32[8,2,32,64]{3,2,1,0:T(8,128)}, u32[]{:S(2)}) copy-start(f32[8,2,32,64]{3,2,1,0:T(8,128)} %u_ref.1) | copy-start | bytes 393220
  1.6 0.9 %copy-start.1 = (bf16[1024,128]{1,0:T(8,128)(2,1)S(1)}, bf16[1024,128]{1,0:T(8,128)(2,1)}, u32[]{:S(2)}) copy-start(bf16[1024,128]{1,0:T(8,128)(2,1)} %bx_ref.1) | copy-start | bytes 786436
  2.5 0.9 %copy-start.2 = (bf16[1024,128]{1,0:T(8,128)(2,1)S(1)}, bf16[1024,128]{1,0:T(8,128)(2,1)}, u32[]{:S(2)}) copy-start(bf16[1024,128]{1,0:T(8,128)(2,1)} %by_ref.1) | copy-start | bytes 786436
  3.5 0.7 copy-start.3
  4.2 0.7 copy-start.4
  4.9 0.7 copy-start.5

commit v2 on v1

--- a/solution.py
+++ b/solution.py
@@ -46,11 +46,13 @@
 
 
 def kernel(
-    u_ref, diff_ref, vel_ref, coup_ref, bx_ref, by_ref,
-    uo_ref, gx_ref, gy_ref, core_ref,
+    u_hbm, diff_hbm, vel_hbm, coup_hbm, bx_hbm, by_hbm,
+    uo_hbm, gx_hbm, gy_hbm, core_hbm,
+    uo_ref, gx_ref, gy_ref, core_ref, s_out,
+    u_ref, diff_ref, vel_ref, coup_ref, bx_ref, by_ref, s_in,
     w, el, er, hl, hr, v, base, acc, th,
-    a_ref, gyb, gzb, ct, ra, pbx, rb, pf, rp, pd, gh, gxb, ds, rd, pby, rdb, cot, rc, et, bxt, byt,
-    s_halo, r_halo, s_yc, r_yc, s_zc, r_zc, s_pz, r_pz, s_zh, r_zh, s_px, r_px,
+    a_ref, gyb, gzb, ct, ra, pbx, rb, pf, ry, pz, rp, pd, gh, gxb, ds, rd, pby, rdb, cot, rc, et, bxt, byt,
+    s_halo, r_halo, s_yc, r_yc, s_zc, r_zc, s_py, r_py, s_pz, r_pz, s_zh, r_zh, s_px, r_px,
     s_ra, r_ra, s_rb, r_rb, s_rd, r_rd, s_rdb, r_rdb, s_co, r_co,
 ):
     sim = lax.axis_index("sim")
@@ -75,7 +77,7 @@
 
     pairs = [(d, e) for d in range(Q) for e in range(2) if (d, e) != (0, 0)]
     self_b = zl == zh
-    self_d = (x == y) & (c == zl // 2)
+    self_d = x == y
 
     barrier = pltpu.get_barrier_semaphore()
 
@@ -97,9 +99,19 @@
         def _():
             tell(dev(zh, y, c, k, x))
 
-        @pl.when(~(self_d & (k == zl)))
-        def _():
-            tell(dev(k, x, zl // 2, zh, y))
+        for e in range(2):
+            @pl.when(~(self_d & (k == y) & (c == e)))
+            def _():
+                tell(dev(zl, k, e, zh, y))
+
+    inputs = [
+        pltpu.make_async_copy(src, dst, s_in.at[i])
+        for i, (src, dst) in enumerate(
+            [(u_hbm, u_ref), (diff_hbm, diff_ref), (vel_hbm, vel_ref), (coup_hbm, coup_ref), (bx_hbm, bx_ref), (by_hbm, by_ref)]
+        )
+    ]
+    for copy in inputs:
+        copy.start()
 
     sends = []
 
@@ -118,6 +130,7 @@
     def lane(shape):
         return lax.broadcasted_iota(jnp.int32, shape, len(shape) - 1)
 
+    inputs[0].wait()
     zero = jnp.zeros((XR, LANES), F32)
     lane32 = lane((XR, LANES))
     left = zero
@@ -133,7 +146,7 @@
     el[...] = left
     er[...] = right
 
-    out_count = jnp.int32(8 + 7 + 6 + 3 + 7 + 2 * Q) - self_b.astype(jnp.int32) - self_d.astype(jnp.int32)
+    out_count = jnp.int32(8 + 7 + 6 + 3 + 7 + 3 * Q) - self_b.astype(jnp.int32) - self_d.astype(jnp.int32)
     pl.semaphore_wait(barrier, out_count)
 
     def halo_sem(dx, dy):
@@ -155,9 +168,15 @@
         i = halo_sem(dx, dy)
         send(src, dst, s_halo.at[i], r_halo.at[i], halo_dev(dx, dy))
 
-    bxt[...] = bx_ref[pl.ds(pl.multiple_of(zl * 256, 256), 256), :].astype(F32).T.astype(BF16)
+    for copy in inputs[1:]:
+        copy.wait()
+    bxt[...] = bx_ref[pl.ds(pl.multiple_of((zl * Q + y) * 2 * XR, 2 * XR), 2 * XR), :].astype(F32).T.astype(BF16)
     byt[...] = jnp.concatenate(
-        [by_ref[pl.ds(pl.multiple_of((k * Q + x) * YC, YC), YC), :].astype(F32) for k in range(Q)], axis=0
+        [
+            by_ref[pl.ds(pl.multiple_of((k * Q + x) * YC + h * 32, 32), 32), :].astype(F32)
+            for h in range(2) for k in range(Q)
+        ],
+        axis=0,
     ).T.astype(BF16)
 
     for dx, dy, src, dst in halo_plan:
@@ -223,42 +242,79 @@
 
     me_yc = y * 2 + c
     me_zc = c * Q + zl
-    for d, e in pairs:
+
+    def send_rows_y(d, e):
         ty, tc = cyc(y, d), c ^ e
         send(a_ref.at[pl.ds(tc * HF, HF)], gyb.at[me_yc], s_yc.at[d * 2 + e], r_yc.at[me_yc], dev(zl, ty, tc, zh, x))
+
+    def rows_y(d, e):
+        sy, sc = cyc(y, -d), c ^ e
+        i = sy * 2 + sc
+        arrive(gyb.at[i], s_yc.at[d * 2 + e], r_yc.at[i], dev(zl, sy, sc, zh, x))
+
+    send_rows_y(0, 1)
     for d, e in pairs:
         if d:
             tz, tc = cyc(zl, d), c ^ e
             send(a_ref.at[pl.ds(tc * HF, HF)], gzb.at[me_zc], s_zc.at[d * 2 + e], r_zc.at[me_zc], dev(tz, y, tc, zh, x))
+    gyb[me_yc] = a_ref[pl.ds(c * HF, HF)]
+    rows_y(0, 1)
+
+    own = jnp.concatenate(
+        [jnp.concatenate([gyb[y * 2, f], gyb[y * 2 + 1, f]], axis=0) for f in range(HF)], axis=1
+    )
+    oh, ol = split(own)
+    part = dot(bxt[...], oh, NN) + dot(bxt[...], ol, NN)
+    for k in range(Q):
+        for j in range(Q):
+            for f in range(HF):
+                pf[k, j, f] = part[j * 32 + k * 8:j * 32 + k * 8 + 8, f * LANES:(f + 1) * LANES]
+    for d in range(1, Q):
+        ty = cyc(y, d)
+        send(pf.at[ty], ry.at[y], s_py.at[d], r_py.at[y], dev(zl, ty, c, zh, x))
+    for d, e in pairs:
+        if d:
+            send_rows_y(d, e)
+    ry[y] = pf[y]
     for f in range(NF):
         for z in range(NZ):
             uo_ref[f, z] = base[f, z, 0:XR, 0:YC]
-    gyb[me_yc] = a_ref[pl.ds(c * HF, HF)]
-
-    for d, e in pairs:
-        sy, sc = cyc(y, -d), c ^ e
-        i = sy * 2 + sc
-        arrive(gyb.at[i], s_yc.at[d * 2 + e], r_yc.at[i], dev(zl, sy, sc, zh, x))
+    outputs = [
+        pltpu.make_async_copy(src, dst, s_out.at[i])
+        for i, (src, dst) in enumerate([(uo_ref, uo_hbm), (gx_ref, gx_hbm), (gy_ref, gy_hbm), (core_ref, core_hbm)])
+    ]
+    outputs[0].start()
+    for e in range(2):
+        gzb[e * Q + zl] = gyb[y * 2 + e]
+    for d in range(1, Q):
+        sy = cyc(y, -d)
+        arrive(ry.at[sy], s_py.at[d], r_py.at[sy], dev(zl, sy, c, zh, x))
+    pz[...] = (ry[0] + ry[1]) + (ry[2] + ry[3])
+    for d in range(1, Q):
+        tz = cyc(zl, d)
+        send(pz.at[tz], rp.at[zl], s_pz.at[d], r_pz.at[zl], dev(tz, y, c, zh, x))
+    rp[zl] = pz[zl]
+    for d in range(1, Q):
+        sz = cyc(zl, -d)
+        arrive(rp.at[sz], s_pz.at[d], r_pz.at[sz], dev(sz, y, c, zh, x))
+    own = (rp[0] + rp[1]) + (rp[2] + rp[3])
+    pd[...] = own
+    for d in range(1, Q):
+        th_ = cyc(zh, d)
+        send(pd, gh.at[zh], s_zh.at[d], r_zh.at[zh], dev(zl, y, c, th_, x))
+    for d in range(1, Q):
+        tx = cyc(x, d)
+        send(pd, gxb.at[x], s_px.at[d], r_px.at[x], dev(zl, y, c, zh, tx))
+    gh[zh] = own
+    gxb[x] = own
 
     def wide(ref):
         return jnp.concatenate([ref[:, f].reshape(2 * Q * XR, LANES) for f in range(HF)], axis=1)
 
-    gyw = wide(gyb)
-    gyh, gyl = split(gyw)
-    part = dot(bxt[...], gyh, NN) + dot(bxt[...], gyl, NN)
-    for f in range(HF):
-        pf[f] = part[:, f * LANES:(f + 1) * LANES]
-
-    def rank_rows(z_):
-        return pl.ds(pl.multiple_of(z_ * 32 + y * 8, 8), 8)
-
-    for d in range(1, Q):
-        tz = cyc(zl, d)
-        send(pf.at[:, rank_rows(tz)], rp.at[zl], s_pz.at[d], r_pz.at[zl], dev(tz, y, c, zh, x))
-    rp[zl] = pf[:, rank_rows(zl), :]
-    for e in range(2):
-        gzb[e * Q + zl] = gyb[y * 2 + e]
-
+    for d, e in pairs:
+        if d:
+            rows_y(d, e)
+    gyh, gyl = split(wide(gyb))
     for d, e in pairs:
         if d:
             sz, sc = cyc(zl, -d), c ^ e
@@ -275,32 +331,28 @@
         send(ct.at[tx, tc], ra.at[me_xc], s_ra.at[d * 2 + e], r_ra.at[me_xc], dev(zl, y, tc, zh, tx))
     ra[me_xc] = ct[x, c]
 
-    for d in range(1, Q):
-        sz = cyc(zl, -d)
-        arrive(rp.at[sz], s_pz.at[d], r_pz.at[sz], dev(sz, y, c, zh, x))
-    own = (rp[0] + rp[1]) + (rp[2] + rp[3])
-    pd[...] = own
-    for d in range(1, Q):
-        th_ = cyc(zh, d)
-        send(pd, gh.at[zh], s_zh.at[d], r_zh.at[zh], dev(zl, y, c, th_, x))
-    for d in range(1, Q):
-        tx = cyc(x, d)
-        send(pd, gxb.at[x], s_px.at[d], r_px.at[x], dev(zl, y, c, zh, tx))
-    gh[zh] = own
-    gxb[x] = own
-
     for d, e in pairs:
         sx, sc = cyc(x, -d), c ^ e
         i = sx * 2 + sc
         arrive(ra.at[i], s_ra.at[d * 2 + e], r_ra.at[i], dev(zl, y, sc, zh, sx))
-    total = ra[0]
-    for i in range(1, 2 * Q):
-        total = total + ra[i]
-    turned = jnp.concatenate([total, total], axis=0).T
     low16 = lane((16, LANES)) < YC
+
+    def fold(parts, out):
+        total = parts[0]
+        for i in range(1, 2 * Q):
+            total = total + parts[i]
+        turned = jnp.concatenate([total, total], axis=0).T
+        for k in range(Q):
+            out[k] = jnp.where(low16, turned[k * 32:k * 32 + 16], turned[k * 32 + 16:k * 32 + 32])
+
+    def unfold(parts, out, scale):
+        gsum = ((parts[0] + parts[1]) + (parts[2] + parts[3])) * scale
+        out[0:16, :] = gsum[:, 0:YC]
+        out[16:32, :] = pltpu.roll(gsum, YC, 1)[:, 0:YC]
+
+    fold(ra, pbx)
     late = []
     for k in range(Q):
-        pbx[k] = jnp.where(low16, turned[k * 32:k * 32 + 16], turned[k * 32 + 16:k * 32 + 32])
         same = self_b & (k == zl)
         copy = pltpu.make_async_remote_copy(
             src_ref=pbx.at[k], dst_ref=rb.at[zh], send_sem=s_rb.at[k], recv_sem=r_rb.at[zh],
@@ -328,7 +380,23 @@
         second = jnp.concatenate([jnp.where(low, r[0], g[1]), jnp.where(low, r[2], g[3])], axis=1)
         return jnp.concatenate([first, second], axis=0)
 
-    cols = unpack(gh)
+    def unpack_halves(ref):
+        g = [ref[k].reshape(32, LANES) for k in range(Q)]
+        quarter = lane((32, LANES)) // 32
+        layers = []
+        for z in range(NZ):
+            halves = []
+            for h in range(2):
+                out = g[0]
+                for k in range(Q):
+                    shift = (k * 32 - z * 64 - h * 32) % LANES
+                    moved = pltpu.roll(g[k], shift, 1) if shift else g[k]
+                    out = moved if k == 0 else jnp.where(quarter == k, moved, out)
+                halves.append(out)
+            layers.append(jnp.concatenate(halves, axis=1))
+        return jnp.concatenate(layers, axis=0)
+
+    cols = unpack_halves(gh)
     ch, cl = split(cols)
     two_h = jnp.concatenate([ch, ch], axis=0)
     two_l = jnp.concatenate([cl, cl], axis=0)
@@ -350,51 +418,40 @@
     for k in range(Q):
         for e in range(2):
             ds[k, e] = dd[k * YC:(k + 1) * YC, e * LANES:(e + 1) * LANES]
-    for d, e in pairs:
-        ty, tc = cyc(y, d), c ^ e
-        send(ds.at[ty, tc], rd.at[me_yc], s_rd.at[d * 2 + e], r_rd.at[me_yc], dev(zl, ty, tc, zh, x))
-    rd[me_yc] = ds[y, c]
+    for k in range(Q):
+        for h in range(2):
+            same = self_d & (k == x) & (c == h)
+            copy = pltpu.make_async_remote_copy(
+                src_ref=ds.at[k, h], dst_ref=rd.at[me_yc], send_sem=s_rd.at[k * 2 + h], recv_sem=r_rd.at[me_yc],
+                device_id=dev(zl, x, h, zh, k), device_id_type=MESH,
+            )
+            late.append((same, copy))
+
+            @pl.when(same)
+            def _():
+                rd[me_yc] = ds[k, h]
+
+            @pl.when(~same)
+            def _():
+                copy.start()
 
     for k in range(Q):
         @pl.when(~(self_b & (k == zh)))
         def _():
             arrive(rb.at[k], s_rb.at[k], r_rb.at[k], dev(zh, y, c, k, x))
-    gsum = ((rb[0] + rb[1]) + (rb[2] + rb[3])) * (1.0 / (NF * NZ * NY))
-    gx_ref[0:16, :] = gsum[:, 0:YC]
-    gx_ref[16:32, :] = pltpu.roll(gsum, YC, 1)[:, 0:YC]
-
-    for d, e in pairs:
-        sy, sc = cyc(y, -d), c ^ e
-        i = sy * 2 + sc
-        arrive(rd.at[i], s_rd.at[d * 2 + e], r_rd.at[i], dev(zl, sy, sc, zh, x))
-    total = rd[0]
-    for i in range(1, 2 * Q):
-        total = total + rd[i]
-    lane16 = lane((16, LANES))
-    for k in range(2):
-        for h in range(2):
-            packed = jnp.zeros((16, LANES), F32)
-            for j in range(4):
-                piece = total[j * 16:(j + 1) * 16]
-                shift = (j * 32 - k * 64 - h * 32) % LANES
-                piece = pltpu.roll(piece, shift, 1) if shift else piece
-                packed = jnp.where(lane16 // 32 == j, piece, packed)
-            m = k * 2 + h
-            pby[m] = packed
-            same = self_d & (2 * c + k == zl) & (c == h)
-            copy = pltpu.make_async_remote_copy(
-                src_ref=pby.at[m], dst_ref=rdb.at[zl], send_sem=s_rdb.at[m], recv_sem=r_rdb.at[zl],
-                device_id=dev(2 * c + k, x, h, zh, y), device_id_type=MESH,
-            )
-            late.append((same, copy))
-
-            @pl.when(same)
+    unfold(rb, gx_ref, 1.0 / (NF * NZ * NY))
+    outputs[1].start()
+
+    for k in range(Q):
+        for e in range(2):
+            @pl.when(~(self_d & (k == y) & (c == e)))
             def _():
-                rdb[zl] = pby[m]
-
-            @pl.when(~same)
-            def _():
-                copy.start()
+                arrive(rd.at[k * 2 + e], s_rd.at[k * 2 + e], r_rd.at[k * 2 + e], dev(zl, k, e, zh, y))
+    fold(rd, pby)
+    for d in range(1, Q):
+        tz = cyc(zl, d)
+        send(pby.at[tz], rdb.at[zl], s_rdb.at[d], r_rdb.at[zl], dev(tz, y, c, zh, x))
+    rdb[zl] = pby[zl]
 
     for d, e in pairs:
         sx, sc = cyc(x, -d), c ^ e
@@ -410,14 +467,16 @@
                 at = fh * 64 + z * 32 + f * 8
                 core_ref[fh * HF + f, z] = jnp.where(c == 0, et[at:at + 4, 0:8], et[at + 4:at + 8, 0:8])
 
-    for k in range(Q):
-        @pl.when(~(self_d & (k == zl)))
-        def _():
-            arrive(rdb.at[k], s_rdb.at[k], r_rdb.at[k], dev(k, x, zl // 2, zh, y))
-    gsum = ((rdb[0] + rdb[1]) + (rdb[2] + rdb[3])) * (1.0 / (NF * NZ * RANK))
-    for j in range(4):
-        gy_ref[j * 16:(j + 1) * 16, :] = (pltpu.roll(gsum, LANES - j * 32, 1) if j else gsum)[:, 0:32]
-
+    outputs[3].start()
+
+    for d in range(1, Q):
+        sz = cyc(zl, -d)
+        arrive(rdb.at[sz], s_rdb.at[d], r_rdb.at[sz], dev(sz, y, c, zh, x))
+    unfold(rdb, gy_ref, 1.0 / (NF * NZ * RANK))
+    outputs[2].start()
+
+    for copy in outputs:
+        copy.wait()
     for copy in sends:
         copy.wait_send()
     for same, copy in late:
@@ -426,40 +485,68 @@
             copy.wait_send()
 
 
+def place(a, b, c, d, ao, bo, co, do, av, bv, cv, dv, sem):
+    into = [pltpu.make_async_copy(src, dst, sem.at[i]) for i, (src, dst) in enumerate([(a, av), (b, bv), (c, cv), (d, dv)])]
+    out = [
+        pltpu.make_async_copy(src, dst, sem.at[4 + i]) for i, (src, dst) in enumerate([(av, ao), (bv, bo), (cv, co), (dv, do)])
+    ]
+    for copy in into:
+        copy.start()
+    for first, second in zip(into, out):
+        first.wait()
+        second.start()
+    for copy in out:
+        copy.wait()
+
+
 def shards(fields, diffusivity, velocity, coupling, basis_x, basis_y):
     vm = lambda *shape: pltpu.VMEM(shape, F32)
     dma = lambda n: pltpu.SemaphoreType.DMA((n,))
-    vspec = pl.BlockSpec(memory_space=pltpu.VMEM)
-    sspec = pl.BlockSpec(memory_space=pltpu.SMEM)
+    hspec = pl.BlockSpec(memory_space=pl.ANY)
+    sm = lambda *shape: pltpu.SMEM(shape, F32)
     scratch = [
+        vm(NF, NZ, XR, YC), vm(XR, YC), vm(XR, YC), vm(NF, NZ, 4, 8), dma(4),
+        vm(NF, NZ, XR, YC), sm(NF), sm(2, NF), sm(NF, NF),
+        pltpu.VMEM((NX, RANK), BF16), pltpu.VMEM((NY, RANK), BF16), dma(6),
         vm(NF * NZ, ROWS, LANES), vm(XR, LANES), vm(XR, LANES), vm(ROWS, LANES), vm(ROWS, LANES),
         vm(NF, NZ, ROWS, LANES), vm(NF, NZ, ROWS, LANES), vm(NF, NZ, ROWS, LANES), vm(2, NF, NZ, ROWS, LANES),
         vm(NF, XR, LANES),
         vm(2 * Q, HF, XR, LANES), vm(2 * Q, HF, XR, LANES),
         vm(Q, 2, YC, LANES), vm(2 * Q, YC, LANES), vm(Q, 16, LANES), vm(Q, 16, LANES),
-        vm(HF, RANK, LANES), vm(Q, HF, 8, LANES), vm(HF, 8, LANES),
+        vm(Q, Q, HF, 8, LANES), vm(Q, Q, HF, 8, LANES), vm(Q, HF, 8, LANES),
+        vm(Q, HF, 8, LANES), vm(HF, 8, LANES),
         vm(Q, HF, 8, LANES), vm(Q, HF, 8, LANES),
         vm(Q, 2, YC, LANES), vm(2 * Q, YC, LANES), vm(Q, 16, LANES), vm(Q, 16, LANES),
         vm(RANK, LANES), vm(2 * Q, 8, LANES), vm(LANES, LANES),
-        pltpu.VMEM((RANK, 256), BF16), pltpu.VMEM((RANK, 256), BF16),
-        dma(9), dma(9), dma(8), dma(8), dma(8), dma(8), dma(4), dma(4), dma(4), dma(4), dma(4), dma(4),
+        pltpu.VMEM((RANK, 2 * XR), BF16), pltpu.VMEM((RANK, 256), BF16),
+        dma(9), dma(9), dma(8), dma(8), dma(8), dma(8), dma(4), dma(4), dma(4), dma(4), dma(4), dma(4), dma(4), dma(4),
         dma(8), dma(8), dma(4), dma(4), dma(8), dma(8), dma(4), dma(4), dma(8), dma(8),
     ]
-    return pl.pallas_call(
+    shapes = (
+        jax.ShapeDtypeStruct((NF, NZ, XR, YC), F32),
+        jax.ShapeDtypeStruct((XR, YC), F32),
+        jax.ShapeDtypeStruct((XR, YC), F32),
+        jax.ShapeDtypeStruct((NF, NZ, 4, 8), F32),
+    )
+    parts = pl.pallas_call(
         kernel,
-        out_shape=(
-            jax.ShapeDtypeStruct((NF, NZ, XR, YC), F32),
-            jax.ShapeDtypeStruct((XR, YC), F32),
-            jax.ShapeDtypeStruct((YC, XR), F32),
-            jax.ShapeDtypeStruct((NF, NZ, 4, 8), F32),
-        ),
-        in_specs=[vspec, sspec, sspec, sspec, vspec, vspec],
-        out_specs=(vspec, vspec, vspec, vspec),
+        out_shape=shapes,
+        in_specs=[hspec] * 6,
+        out_specs=(hspec,) * 4,
         scratch_shapes=scratch,
         compiler_params=pltpu.CompilerParams(
-            collective_id=0, has_side_effects=True, vmem_limit_bytes=40 * 1024 * 1024
+            collective_id=0, has_side_effects=True, vmem_limit_bytes=63 * 1024 * 1024
         ),
     )(fields, diffusivity, velocity, coupling, basis_x, basis_y)
+    state, gram_x, gram_y, core = pl.pallas_call(
+        place,
+        out_shape=shapes,
+        in_specs=[hspec] * 4,
+        out_specs=(hspec,) * 4,
+        scratch_shapes=[vm(NF, NZ, XR, YC), vm(XR, YC), vm(XR, YC), vm(NF, NZ, 4, 8), dma(8)],
+        compiler_params=pltpu.CompilerParams(vmem_limit_bytes=63 * 1024 * 1024),
+    )(*parts)
+    return state, gram_x, gram_y.T, core
 
 
 def solution(mesh):

time: 73.9 us -> 67.2 us (0.909)
  local copies, waits for them, and re-layouts: 7.46 us -> 0 us
    unnamed x15 -> x0, local copies, waits for them, and re-layouts: 6.78 us -> none
    pallas_call x1 -> x2, Pallas kernels: 65.5 us -> 66.1 us  [the longest x1 64.4 us: shards(): pl.pallas_call(kernel, out_shape=shapes, in_specs=[hspec] * 6, out_specs=...]
where the time goes in v2:
time: 67.2 us; the launch traced here: 66.8 us
  Pallas kernels  66.1 us (98%)
    pallas_call x1, Pallas kernels, shards(): pl.pallas_call(kernel, out_shape=shapes, in_specs=[hspec] * 6, out_specs=...  64.4 us
    pallas_call x1, Pallas kernels, shards(): pl.pallas_call(place, out_shape=shapes, in_specs=[hspec] * 4, out_specs=(...  1.73 us

profile of v2, /device:TPU:1, one launch (start us, length us, event | category | flops | bytes accessed | tf_op | source)
XLA Modules:
  0.0 66.8 jit_solution(3590859347745937181)
XLA Ops:
  0.6 64.4 %shard_map.93 = (f32[8,2,32,64]{3,2,1,0:T(8,128)}, f32[32,64]{1,0:T(8,128)}, f32[32,64]{1,0:T(8,128)}, f32[8,2,4,8]{3,2,1,0:T(4,128)}) custom-call(f32[8,2,32,64]{3,2,1,0:T(8,128)} %u_hbm.1, f32[8]{0:T(128)} %diff_hbm.1, f32[2,8]{1,0:T(2,128)} %vel_hbm.1, f32[8,8]{1,0:T(8,128)} %coup_hbm.1, bf16[1024,128]{1,0:T(8,128)(2,1)} %bx_hbm.1, bf16[1024,128]{1,0:T(8,128)(2,1)} %by_hbm.1), custom_call_target="tpu_custom_call" | custom-call | tf_op jit(solution)/shard_map/pallas_call | solution.py:531
  65.0 1.7 %shard_map.94 = (f32[8,2,32,64]{3,2,1,0:T(8,128)}, f32[32,64]{1,0:T(8,128)}, f32[32,64]{1,0:T(8,128)}, f32[8,2,4,8]{3,2,1,0:T(4,128)}) custom-call(f32[8,2,32,64]{3,2,1,0:T(8,128)} %get-tuple-element.12.a, f32[32,64]{1,0:T(8,128)} %get-tuple-element.13.b, f32[32,64]{1,0:T(8,128)} %get-tuple-element.14.c, f32[8,2,4,8]{3,2,1,0:T(4,128)} %get-tuple-element.15.d), custom_call_target="tpu_custom_call" | custom-call | tf_op jit(solution)/shard_map/pallas_call | solution.py:541

commit v3 on v2

--- a/solution.py
+++ b/solution.py
@@ -198,7 +198,7 @@
         for stage in range(4):
             now, later = stage % 2, (stage + 1) % 2
 
-            def field(f, carry2):
+            for f in range(NF):
                 d = diff_ref[f]
                 vx = vel_ref[0, f] * 0.5
                 vy = vel_ref[1, f] * 0.5
@@ -229,9 +229,6 @@
                         base[f, z] = new
                     v[f, z] = new
                     th[later, f, z] = jnp.tanh(new)
-                return carry2
-
-            lax.fori_loop(0, NF, field, 0)
         return carry
 
     lax.fori_loop(0, STEPS, step, 0)

time: 67.2 us -> 64.2 us (0.955)
  Pallas kernels: 66.1 us -> 63.2 us
    pallas_call x1, Pallas kernels: 64.4 us -> 61.5 us  [shards(): pl.pallas_call(kernel, out_shape=shapes, in_specs=[hspec] * 6, out_specs=...]
where the time goes in v3:
time: 64.2 us; the launch traced here: 63.8 us
  Pallas kernels  63.2 us (98%)
    pallas_call x1, Pallas kernels, shards(): pl.pallas_call(kernel, out_shape=shapes, in_specs=[hspec] * 6, out_specs=...  61.5 us
    pallas_call x1, Pallas kernels, shards(): pl.pallas_call(place, out_shape=shapes, in_specs=[hspec] * 4, out_specs=(...  1.73 us

profile of v3, /device:TPU:1, one launch (start us, length us, event | category | flops | bytes accessed | tf_op | source)
XLA Modules:
  0.0 63.8 jit_solution(17417007012962305711)
XLA Ops:
  0.6 61.5 %shard_map.93 = (f32[8,2,32,64]{3,2,1,0:T(8,128)}, f32[32,64]{1,0:T(8,128)}, f32[32,64]{1,0:T(8,128)}, f32[8,2,4,8]{3,2,1,0:T(4,128)}) custom-call(f32[8,2,32,64]{3,2,1,0:T(8,128)} %u_hbm.1, f32[8]{0:T(128)} %diff_hbm.1, f32[2,8]{1,0:T(2,128)} %vel_hbm.1, f32[8,8]{1,0:T(8,128)} %coup_hbm.1, bf16[1024,128]{1,0:T(8,128)(2,1)} %bx_hbm.1, bf16[1024,128]{1,0:T(8,128)(2,1)} %by_hbm.1), custom_call_target="tpu_custom_call" | custom-call | tf_op jit(solution)/shard_map/pallas_call | solution.py:528
  62.1 1.7 %shard_map.94 = (f32[8,2,32,64]{3,2,1,0:T(8,128)}, f32[32,64]{1,0:T(8,128)}, f32[32,64]{1,0:T(8,128)}, f32[8,2,4,8]{3,2,1,0:T(4,128)}) custom-call(f32[8,2,32,64]{3,2,1,0:T(8,128)} %get-tuple-element.12.a, f32[32,64]{1,0:T(8,128)} %get-tuple-element.13.b, f32[32,64]{1,0:T(8,128)} %get-tuple-element.14.c, f32[8,2,4,8]{3,2,1,0:T(4,128)} %get-tuple-element.15.d), custom_call_target="tpu_custom_call" | custom-call | tf_op jit(solution)/shard_map/pallas_call | solution.py:538

commit v4 on v3

--- a/solution.py
+++ b/solution.py
@@ -51,8 +51,8 @@
     uo_ref, gx_ref, gy_ref, core_ref, s_out,
     u_ref, diff_ref, vel_ref, coup_ref, bx_ref, by_ref, s_in,
     w, el, er, hl, hr, v, base, acc, th,
-    a_ref, gyb, gzb, ct, ra, pbx, rb, pf, ry, pz, rp, pd, gh, gxb, ds, rd, pby, rdb, cot, rc, et, bxt, byt,
-    s_halo, r_halo, s_yc, r_yc, s_zc, r_zc, s_py, r_py, s_pz, r_pz, s_zh, r_zh, s_px, r_px,
+    a_ref, gyb, gzb, ct, ra, pbx, rb, pf, ry, pz, rp, pd, gh, gxb, gh2, gx2, ds, rd, pby, rdb, cot, rc, et, bxt, byt,
+    s_halo, r_halo, s_yc, r_yc, s_zc, r_zc, s_py, r_py, s_pz, r_pz, s_zh, r_zh, s_px, r_px, s_fh, r_fh, s_fx, r_fx,
     s_ra, r_ra, s_rb, r_rb, s_rd, r_rd, s_rdb, r_rdb, s_co, r_co,
 ):
     sim = lax.axis_index("sim")
@@ -87,23 +87,6 @@
     halo_dirs = [(dx, dy) for dx in (-1, 0, 1) for dy in (-1, 0, 1) if (dx, dy) != (0, 0)]
     for dx, dy in halo_dirs:
         tell(halo_dev(dx, dy))
-    for d, e in pairs:
-        tell(dev(zl, cyc(y, -d), c ^ e, zh, x))
-        tell(dev(zl, y, c ^ e, zh, cyc(x, -d)))
-        if d:
-            tell(dev(cyc(zl, -d), y, c ^ e, zh, x))
-    for d in range(1, Q):
-        tell(dev(zl, y, c, cyc(zh, -d), x))
-    for k in range(Q):
-        @pl.when(~(self_b & (k == zh)))
-        def _():
-            tell(dev(zh, y, c, k, x))
-
-        for e in range(2):
-            @pl.when(~(self_d & (k == y) & (c == e)))
-            def _():
-                tell(dev(zl, k, e, zh, y))
-
     inputs = [
         pltpu.make_async_copy(src, dst, s_in.at[i])
         for i, (src, dst) in enumerate(
@@ -112,6 +95,21 @@
     ]
     for copy in inputs:
         copy.start()
+    for d, e in pairs:
+        tell(dev(zl, cyc(y, -d), c ^ e, zh, x))
+        tell(dev(zl, y, c ^ e, zh, cyc(x, -d)))
+        if d:
+            tell(dev(cyc(zl, -d), y, c ^ e, zh, x))
+    for d in range(1, Q):
+        tell(dev(zl, y, c, cyc(zh, -d), x))
+    for k in range(Q):
+        @pl.when(~(self_b & (k == zh)))
+        def _():
+            tell(dev(zh, y, c, k, x))
+
+        @pl.when(~(self_d & (k == y)))
+        def _():
+            tell(dev(zl, k, c, zh, y))
 
     sends = []
 
@@ -146,7 +144,7 @@
     el[...] = left
     er[...] = right
 
-    out_count = jnp.int32(8 + 7 + 6 + 3 + 7 + 3 * Q) - self_b.astype(jnp.int32) - self_d.astype(jnp.int32)
+    out_count = jnp.int32(8 + 7 + 6 + 3 + 7 + 2 * Q) - self_b.astype(jnp.int32) - self_d.astype(jnp.int32)
     pl.semaphore_wait(barrier, out_count)
 
     def halo_sem(dx, dy):
@@ -302,6 +300,9 @@
     for d in range(1, Q):
         tx = cyc(x, d)
         send(pd, gxb.at[x], s_px.at[d], r_px.at[x], dev(zl, y, c, zh, tx))
+    sibling = dev(zl, y, c ^ 1, zh, x)
+    send(pd, gx2.at[x], s_fx.at[0], r_fx.at[x], sibling)
+    send(pd, gh2.at[zh], s_fh.at[0], r_fh.at[zh], sibling)
     gh[zh] = own
     gxb[x] = own
 
@@ -328,15 +329,90 @@
         send(ct.at[tx, tc], ra.at[me_xc], s_ra.at[d * 2 + e], r_ra.at[me_xc], dev(zl, y, tc, zh, tx))
     ra[me_xc] = ct[x, c]
 
+    late = []
+    low = lane((32, LANES)) < YC
+
+    def unpack(ref):
+        g = [ref[k].reshape(32, LANES) for k in range(Q)]
+        r = [pltpu.roll(t, YC, 1) for t in g]
+        first = jnp.concatenate([jnp.where(low, g[0], r[1]), jnp.where(low, g[2], r[3])], axis=1)
+        second = jnp.concatenate([jnp.where(low, r[0], g[1]), jnp.where(low, r[2], g[3])], axis=1)
+        return jnp.concatenate([first, second], axis=0)
+
+    quarter = lane((32, LANES)) // 32
+
+    def pack_half(g, h):
+        layers = []
+        for z in range(NZ):
+            out = g[0]
+            for k in range(Q):
+                shift = (k * 32 - z * 64 - h * 32) % LANES
+                moved = pltpu.roll(g[k], shift, 1) if shift else g[k]
+                out = moved if k == 0 else jnp.where(quarter == k, moved, out)
+            layers.append(out)
+        return jnp.concatenate(layers, axis=0)
+
+    for d in range(1, Q):
+        sx = cyc(x, -d)
+        arrive(gxb.at[sx], s_px.at[d], r_px.at[sx], dev(zl, y, c, zh, sx))
+        send(gxb.at[sx], gx2.at[sx], s_fx.at[d], r_fx.at[sx], sibling)
+    for k in range(Q):
+        arrive(gx2.at[k], s_fx.at[k], r_fx.at[k], sibling)
+    rh, rl = split(jnp.concatenate([unpack(gxb), unpack(gx2)], axis=0).T)
+
+    for d in (1, 3, 2):
+        sh = cyc(zh, -d)
+        arrive(gh.at[sh], s_zh.at[d], r_zh.at[sh], dev(zl, y, c, sh, x))
+        send(gh.at[sh], gh2.at[sh], s_fh.at[d], r_fh.at[sh], sibling)
+    mine_g = [gh[k].reshape(32, LANES) for k in range(Q)]
+    halves = [pack_half(mine_g, h) for h in range(2)]
+    for k in range(Q):
+        arrive(gh2.at[k], s_fh.at[k], r_fh.at[k], sibling)
+    other_g = [gh2[k].reshape(32, LANES) for k in range(Q)]
+    other_g = [jnp.where(c == 0, t, pltpu.roll(t, LANES - 32, 1)) for t in other_g]
+    kcols = jnp.concatenate([jnp.where(c == 0, halves[0], halves[1]), pack_half(other_g, 0)], axis=0)
+    kh, kl = split(kcols)
+    dd = dot(rh, kh, NN) + (dot(rh, kl, NN) + dot(rl, kh, NN))
+    for k in range(Q):
+        ds[k] = dd[k * YC:(k + 1) * YC]
+    for k in range(Q):
+        same = self_d & (k == x)
+        copy = pltpu.make_async_remote_copy(
+            src_ref=ds.at[k], dst_ref=rd.at[y], send_sem=s_rd.at[k], recv_sem=r_rd.at[y],
+            device_id=dev(zl, x, c, zh, k), device_id_type=MESH,
+        )
+        late.append((same, copy))
+
+        @pl.when(same)
+        def _():
+            rd[y] = ds[k]
+
+        @pl.when(~same)
+        def _():
+            copy.start()
+
+    ch, cl = split(jnp.concatenate(halves, axis=1))
+    two_h = jnp.concatenate([ch, ch], axis=0)
+    two_l = jnp.concatenate([cl, cl], axis=0)
+    cot[...] = dot(byt[...], two_h, NT) + dot(byt[...], two_l, NT)
+
+    def core_rows(x_):
+        return pl.ds(pl.multiple_of(zh * 32 + x_ * 8, 8), 8)
+
+    for d, e in pairs:
+        tx, tc = cyc(x, d), c ^ e
+        send(cot.at[core_rows(tx)], rc.at[me_xc], s_co.at[d * 2 + e], r_co.at[me_xc], dev(zl, y, tc, zh, tx))
+    rc[me_xc] = cot[core_rows(x), :]
+
     for d, e in pairs:
         sx, sc = cyc(x, -d), c ^ e
         i = sx * 2 + sc
         arrive(ra.at[i], s_ra.at[d * 2 + e], r_ra.at[i], dev(zl, y, sc, zh, sx))
     low16 = lane((16, LANES)) < YC
 
-    def fold(parts, out):
+    def fold(parts, out, count):
         total = parts[0]
-        for i in range(1, 2 * Q):
+        for i in range(1, count):
             total = total + parts[i]
         turned = jnp.concatenate([total, total], axis=0).T
         for k in range(Q):
@@ -347,8 +423,7 @@
         out[0:16, :] = gsum[:, 0:YC]
         out[16:32, :] = pltpu.roll(gsum, YC, 1)[:, 0:YC]
 
-    fold(ra, pbx)
-    late = []
+    fold(ra, pbx, 2 * Q)
     for k in range(Q):
         same = self_b & (k == zl)
         copy = pltpu.make_async_remote_copy(
@@ -365,86 +440,11 @@
         def _():
             copy.start()
 
-    for d in range(1, Q):
-        sh = cyc(zh, -d)
-        arrive(gh.at[sh], s_zh.at[d], r_zh.at[sh], dev(zl, y, c, sh, x))
-    low = lane((32, LANES)) < YC
-
-    def unpack(ref):
-        g = [ref[k].reshape(32, LANES) for k in range(Q)]
-        r = [pltpu.roll(t, YC, 1) for t in g]
-        first = jnp.concatenate([jnp.where(low, g[0], r[1]), jnp.where(low, g[2], r[3])], axis=1)
-        second = jnp.concatenate([jnp.where(low, r[0], g[1]), jnp.where(low, r[2], g[3])], axis=1)
-        return jnp.concatenate([first, second], axis=0)
-
-    def unpack_halves(ref):
-        g = [ref[k].reshape(32, LANES) for k in range(Q)]
-        quarter = lane((32, LANES)) // 32
-        layers = []
-        for z in range(NZ):
-            halves = []
-            for h in range(2):
-                out = g[0]
-                for k in range(Q):
-                    shift = (k * 32 - z * 64 - h * 32) % LANES
-                    moved = pltpu.roll(g[k], shift, 1) if shift else g[k]
-                    out = moved if k == 0 else jnp.where(quarter == k, moved, out)
-                halves.append(out)
-            layers.append(jnp.concatenate(halves, axis=1))
-        return jnp.concatenate(layers, axis=0)
-
-    cols = unpack_halves(gh)
-    ch, cl = split(cols)
-    two_h = jnp.concatenate([ch, ch], axis=0)
-    two_l = jnp.concatenate([cl, cl], axis=0)
-    cot[...] = dot(byt[...], two_h, NT) + dot(byt[...], two_l, NT)
-
-    def core_rows(x_):
-        return pl.ds(pl.multiple_of(zh * 32 + x_ * 8, 8), 8)
-
-    for d, e in pairs:
-        tx, tc = cyc(x, d), c ^ e
-        send(cot.at[core_rows(tx)], rc.at[me_xc], s_co.at[d * 2 + e], r_co.at[me_xc], dev(zl, y, tc, zh, tx))
-    rc[me_xc] = cot[core_rows(x), :]
-
-    for d in range(1, Q):
-        sx = cyc(x, -d)
-        arrive(gxb.at[sx], s_px.at[d], r_px.at[sx], dev(zl, y, c, zh, sx))
-    rh, rl = split(unpack(gxb).T)
-    dd = dot(rh, ch, NN) + (dot(rh, cl, NN) + dot(rl, ch, NN))
-    for k in range(Q):
-        for e in range(2):
-            ds[k, e] = dd[k * YC:(k + 1) * YC, e * LANES:(e + 1) * LANES]
-    for k in range(Q):
-        for h in range(2):
-            same = self_d & (k == x) & (c == h)
-            copy = pltpu.make_async_remote_copy(
-                src_ref=ds.at[k, h], dst_ref=rd.at[me_yc], send_sem=s_rd.at[k * 2 + h], recv_sem=r_rd.at[me_yc],
-                device_id=dev(zl, x, h, zh, k), device_id_type=MESH,
-            )
-            late.append((same, copy))
-
-            @pl.when(same)
-            def _():
-                rd[me_yc] = ds[k, h]
-
-            @pl.when(~same)
-            def _():
-                copy.start()
-
-    for k in range(Q):
-        @pl.when(~(self_b & (k == zh)))
-        def _():
-            arrive(rb.at[k], s_rb.at[k], r_rb.at[k], dev(zh, y, c, k, x))
-    unfold(rb, gx_ref, 1.0 / (NF * NZ * NY))
-    outputs[1].start()
-
-    for k in range(Q):
-        for e in range(2):
-            @pl.when(~(self_d & (k == y) & (c == e)))
-            def _():
-                arrive(rd.at[k * 2 + e], s_rd.at[k * 2 + e], r_rd.at[k * 2 + e], dev(zl, k, e, zh, y))
-    fold(rd, pby)
+    for k in range(Q):
+        @pl.when(~(self_d & (k == y)))
+        def _():
+            arrive(rd.at[k], s_rd.at[k], r_rd.at[k], dev(zl, k, c, zh, y))
+    fold(rd, pby, Q)
     for d in range(1, Q):
         tz = cyc(zl, d)
         send(pby.at[tz], rdb.at[zl], s_rdb.at[d], r_rdb.at[zl], dev(tz, y, c, zh, x))
@@ -465,6 +465,13 @@
                 core_ref[fh * HF + f, z] = jnp.where(c == 0, et[at:at + 4, 0:8], et[at + 4:at + 8, 0:8])
 
     outputs[3].start()
+
+    for k in range(Q):
+        @pl.when(~(self_b & (k == zh)))
+        def _():
+            arrive(rb.at[k], s_rb.at[k], r_rb.at[k], dev(zh, y, c, k, x))
+    unfold(rb, gx_ref, 1.0 / (NF * NZ * NY))
+    outputs[1].start()
 
     for d in range(1, Q):
         sz = cyc(zl, -d)
@@ -512,12 +519,12 @@
         vm(Q, 2, YC, LANES), vm(2 * Q, YC, LANES), vm(Q, 16, LANES), vm(Q, 16, LANES),
         vm(Q, Q, HF, 8, LANES), vm(Q, Q, HF, 8, LANES), vm(Q, HF, 8, LANES),
         vm(Q, HF, 8, LANES), vm(HF, 8, LANES),
-        vm(Q, HF, 8, LANES), vm(Q, HF, 8, LANES),
-        vm(Q, 2, YC, LANES), vm(2 * Q, YC, LANES), vm(Q, 16, LANES), vm(Q, 16, LANES),
+        vm(Q, HF, 8, LANES), vm(Q, HF, 8, LANES), vm(Q, HF, 8, LANES), vm(Q, HF, 8, LANES),
+        vm(Q, YC, LANES), vm(Q, YC, LANES), vm(Q, 16, LANES), vm(Q, 16, LANES),
         vm(RANK, LANES), vm(2 * Q, 8, LANES), vm(LANES, LANES),
         pltpu.VMEM((RANK, 2 * XR), BF16), pltpu.VMEM((RANK, 256), BF16),
-        dma(9), dma(9), dma(8), dma(8), dma(8), dma(8), dma(4), dma(4), dma(4), dma(4), dma(4), dma(4), dma(4), dma(4),
-        dma(8), dma(8), dma(4), dma(4), dma(8), dma(8), dma(4), dma(4), dma(8), dma(8),
+        dma(9), dma(9), dma(8), dma(8), dma(8), dma(8), dma(4), dma(4), dma(4), dma(4), dma(4), dma(4), dma(4), dma(4), dma(4), dma(4), dma(4), dma(4),
+        dma(8), dma(8), dma(4), dma(4), dma(4), dma(4), dma(4), dma(4), dma(8), dma(8),
     ]
     shapes = (
         jax.ShapeDtypeStruct((NF, NZ, XR, YC), F32),

time: 64.2 us -> 63.9 us (level)
  no operation moved by 1% of the time
where the time goes in v4:
time: 63.9 us; the launch traced here: 63.4 us
  Pallas kernels  62.7 us (98%)
  between operations  0.64 us (1%)
    pallas_call x1, Pallas kernels, shards(): pl.pallas_call(kernel, out_shape=shapes, in_specs=[hspec] * 6, out_specs=...  61 us
    pallas_call x1, Pallas kernels, shards(): pl.pallas_call(place, out_shape=shapes, in_specs=[hspec] * 4, out_specs=(...  1.73 us

profile of v4, /device:TPU:1, one launch (start us, length us, event | category | flops | bytes accessed | tf_op | source)
XLA Modules:
  0.0 63.4 jit_solution(16801052733405237479)
XLA Ops:
  0.6 61.0 %shard_map.93 = (f32[8,2,32,64]{3,2,1,0:T(8,128)}, f32[32,64]{1,0:T(8,128)}, f32[32,64]{1,0:T(8,128)}, f32[8,2,4,8]{3,2,1,0:T(4,128)}) custom-call(f32[8,2,32,64]{3,2,1,0:T(8,128)} %u_hbm.1, f32[8]{0:T(128)} %diff_hbm.1, f32[2,8]{1,0:T(2,128)} %vel_hbm.1, f32[8,8]{1,0:T(8,128)} %coup_hbm.1, bf16[1024,128]{1,0:T(8,128)(2,1)} %bx_hbm.1, bf16[1024,128]{1,0:T(8,128)(2,1)} %by_hbm.1), custom_call_target="tpu_custom_call" | custom-call | tf_op jit(solution)/shard_map/pallas_call | solution.py:535
  61.6 1.7 %shard_map.94 = (f32[8,2,32,64]{3,2,1,0:T(8,128)}, f32[32,64]{1,0:T(8,128)}, f32[32,64]{1,0:T(8,128)}, f32[8,2,4,8]{3,2,1,0:T(4,128)}) custom-call(f32[8,2,32,64]{3,2,1,0:T(8,128)} %get-tuple-element.12.a, f32[32,64]{1,0:T(8,128)} %get-tuple-element.13.b, f32[32,64]{1,0:T(8,128)} %get-tuple-element.14.c, f32[8,2,4,8]{3,2,1,0:T(4,128)} %get-tuple-element.15.d), custom_call_target="tpu_custom_call" | custom-call | tf_op jit(solution)/shard_map/pallas_call | solution.py:545

commit v5 on v4

--- a/solution.py
+++ b/solution.py
@@ -360,50 +360,6 @@
         arrive(gx2.at[k], s_fx.at[k], r_fx.at[k], sibling)
     rh, rl = split(jnp.concatenate([unpack(gxb), unpack(gx2)], axis=0).T)
 
-    for d in (1, 3, 2):
-        sh = cyc(zh, -d)
-        arrive(gh.at[sh], s_zh.at[d], r_zh.at[sh], dev(zl, y, c, sh, x))
-        send(gh.at[sh], gh2.at[sh], s_fh.at[d], r_fh.at[sh], sibling)
-    mine_g = [gh[k].reshape(32, LANES) for k in range(Q)]
-    halves = [pack_half(mine_g, h) for h in range(2)]
-    for k in range(Q):
-        arrive(gh2.at[k], s_fh.at[k], r_fh.at[k], sibling)
-    other_g = [gh2[k].reshape(32, LANES) for k in range(Q)]
-    other_g = [jnp.where(c == 0, t, pltpu.roll(t, LANES - 32, 1)) for t in other_g]
-    kcols = jnp.concatenate([jnp.where(c == 0, halves[0], halves[1]), pack_half(other_g, 0)], axis=0)
-    kh, kl = split(kcols)
-    dd = dot(rh, kh, NN) + (dot(rh, kl, NN) + dot(rl, kh, NN))
-    for k in range(Q):
-        ds[k] = dd[k * YC:(k + 1) * YC]
-    for k in range(Q):
-        same = self_d & (k == x)
-        copy = pltpu.make_async_remote_copy(
-            src_ref=ds.at[k], dst_ref=rd.at[y], send_sem=s_rd.at[k], recv_sem=r_rd.at[y],
-            device_id=dev(zl, x, c, zh, k), device_id_type=MESH,
-        )
-        late.append((same, copy))
-
-        @pl.when(same)
-        def _():
-            rd[y] = ds[k]
-
-        @pl.when(~same)
-        def _():
-            copy.start()
-
-    ch, cl = split(jnp.concatenate(halves, axis=1))
-    two_h = jnp.concatenate([ch, ch], axis=0)
-    two_l = jnp.concatenate([cl, cl], axis=0)
-    cot[...] = dot(byt[...], two_h, NT) + dot(byt[...], two_l, NT)
-
-    def core_rows(x_):
-        return pl.ds(pl.multiple_of(zh * 32 + x_ * 8, 8), 8)
-
-    for d, e in pairs:
-        tx, tc = cyc(x, d), c ^ e
-        send(cot.at[core_rows(tx)], rc.at[me_xc], s_co.at[d * 2 + e], r_co.at[me_xc], dev(zl, y, tc, zh, tx))
-    rc[me_xc] = cot[core_rows(x), :]
-
     for d, e in pairs:
         sx, sc = cyc(x, -d), c ^ e
         i = sx * 2 + sc
@@ -439,6 +395,50 @@
         @pl.when(~same)
         def _():
             copy.start()
+
+    for d in (1, 3, 2):
+        sh = cyc(zh, -d)
+        arrive(gh.at[sh], s_zh.at[d], r_zh.at[sh], dev(zl, y, c, sh, x))
+        send(gh.at[sh], gh2.at[sh], s_fh.at[d], r_fh.at[sh], sibling)
+    mine_g = [gh[k].reshape(32, LANES) for k in range(Q)]
+    halves = [pack_half(mine_g, h) for h in range(2)]
+    for k in range(Q):
+        arrive(gh2.at[k], s_fh.at[k], r_fh.at[k], sibling)
+    other_g = [gh2[k].reshape(32, LANES) for k in range(Q)]
+    other_g = [jnp.where(c == 0, t, pltpu.roll(t, LANES - 32, 1)) for t in other_g]
+    kcols = jnp.concatenate([jnp.where(c == 0, halves[0], halves[1]), pack_half(other_g, 0)], axis=0)
+    kh, kl = split(kcols)
+    dd = dot(rh, kh, NN) + (dot(rh, kl, NN) + dot(rl, kh, NN))
+    for k in range(Q):
+        ds[k] = dd[k * YC:(k + 1) * YC]
+    for k in range(Q):
+        same = self_d & (k == x)
+        copy = pltpu.make_async_remote_copy(
+            src_ref=ds.at[k], dst_ref=rd.at[y], send_sem=s_rd.at[k], recv_sem=r_rd.at[y],
+            device_id=dev(zl, x, c, zh, k), device_id_type=MESH,
+        )
+        late.append((same, copy))
+
+        @pl.when(same)
+        def _():
+            rd[y] = ds[k]
+
+        @pl.when(~same)
+        def _():
+            copy.start()
+
+    ch, cl = split(jnp.concatenate(halves, axis=1))
+    two_h = jnp.concatenate([ch, ch], axis=0)
+    two_l = jnp.concatenate([cl, cl], axis=0)
+    cot[...] = dot(byt[...], two_h, NT) + dot(byt[...], two_l, NT)
+
+    def core_rows(x_):
+        return pl.ds(pl.multiple_of(zh * 32 + x_ * 8, 8), 8)
+
+    for d, e in pairs:
+        tx, tc = cyc(x, d), c ^ e
+        send(cot.at[core_rows(tx)], rc.at[me_xc], s_co.at[d * 2 + e], r_co.at[me_xc], dev(zl, y, tc, zh, tx))
+    rc[me_xc] = cot[core_rows(x), :]
 
     for k in range(Q):
         @pl.when(~(self_d & (k == y)))

time: 63.9 us -> 63.9 us (level)
  no operation moved by 1% of the time
where the time goes in v5:
time: 63.9 us; the launch traced here: 63.4 us
  Pallas kernels  62.8 us (98%)
  between operations  0.64 us (1%)
    pallas_call x1, Pallas kernels, shards(): pl.pallas_call(kernel, out_shape=shapes, in_specs=[hspec] * 6, out_specs=...  61.1 us
    pallas_call x1, Pallas kernels, shards(): pl.pallas_call(place, out_shape=shapes, in_specs=[hspec] * 4, out_specs=(...  1.73 us

profile of v5, /device:TPU:1, one launch (start us, length us, event | category | flops | bytes accessed | tf_op | source)
XLA Modules:
  0.0 63.4 jit_solution(12348010949125545765)
XLA Ops:
  0.6 61.1 %shard_map.93 = (f32[8,2,32,64]{3,2,1,0:T(8,128)}, f32[32,64]{1,0:T(8,128)}, f32[32,64]{1,0:T(8,128)}, f32[8,2,4,8]{3,2,1,0:T(4,128)}) custom-call(f32[8,2,32,64]{3,2,1,0:T(8,128)} %u_hbm.1, f32[8]{0:T(128)} %diff_hbm.1, f32[2,8]{1,0:T(2,128)} %vel_hbm.1, f32[8,8]{1,0:T(8,128)} %coup_hbm.1, bf16[1024,128]{1,0:T(8,128)(2,1)} %bx_hbm.1, bf16[1024,128]{1,0:T(8,128)(2,1)} %by_hbm.1), custom_call_target="tpu_custom_call" | custom-call | tf_op jit(solution)/shard_map/pallas_call | solution.py:535
  61.7 1.7 %shard_map.94 = (f32[8,2,32,64]{3,2,1,0:T(8,128)}, f32[32,64]{1,0:T(8,128)}, f32[32,64]{1,0:T(8,128)}, f32[8,2,4,8]{3,2,1,0:T(4,128)}) custom-call(f32[8,2,32,64]{3,2,1,0:T(8,128)} %get-tuple-element.12.a, f32[32,64]{1,0:T(8,128)} %get-tuple-element.13.b, f32[32,64]{1,0:T(8,128)} %get-tuple-element.14.c, f32[8,2,4,8]{3,2,1,0:T(4,128)} %get-tuple-element.15.d), custom_call_target="tpu_custom_call" | custom-call | tf_op jit(solution)/shard_map/pallas_call | solution.py:545
